TPU v7x, 32 devices: a whole 2x2x4 slice. The times are simulated.
32 devices in a mesh: clip: 8 (over z, y), tile: 4 (over x, core).
Axes of the slice: x: 2, y: 2, z: 4, core: 2. Of those that a mesh axis runs over, the one named last changes fastest.
Arguments:
- codes: int32 [8, 16, 256], P('clip', None, 'tile'), may hold values from 0 to 1023
- mask: int32 [8, 16, 256], P('clip', None, 'tile'), may hold values 0 or 1
- actions: int32 [8, 16], P('clip'), may hold values from 0 to 7
- domains: int32 [8], P('clip'), may hold values from 0 to 3
- weights: float32 [1024, 18432], P('clip')
- weight_m: float32 [1024, 18432], P('clip'), may hold values from -0.00015258789 to 0.00015258789
- weight_v: float32 [1024, 18432], P('clip'), may hold values from 2.7842804e-09 to 1.1115948e-08
- stats: float32 [8, 1024, 64], P(None, 'clip'), as said below
- bases: float32 [8, 1024, 64], P(None, 'clip'), as said below
- vectors: float32 [17, 1024], P(None, 'clip')
- vector_m: float32 [17, 1024], P(None, 'clip'), may hold values from -0.00061035156 to 0.00061035156
- vector_v: float32 [17, 1024], P(None, 'clip'), may hold values from 4.4463793e-08 to 1.7997249e-07
Outputs:
- loss_terms: float32 [2, 4], replicated
- grad_norm: float32 [], replicated
- new_weights: float32 [1024, 18432], P('clip')
- new_weight_m: float32 [1024, 18432], P('clip')
- new_weight_v: float32 [1024, 18432], P('clip')
- new_stats: float32 [8, 1024, 64], P(None, 'clip')
- new_bases: float32 [8, 1024, 64], P(None, 'clip')
- new_vectors: float32 [17, 1024], P(None, 'clip')
- new_vector_m: float32 [17, 1024], P(None, 'clip')
- new_vector_v: float32 [17, 1024], P(None, 'clip')
Inputs may be any that keep to these rules, and one draw needn't show every extreme that they name: `stats`: symmetric, diagonally dominant 64 x 64 blocks with positive diagonal. `bases`: each 64 x 64 block is orthonormal.
All inputs are finite; a program needn't handle non-finite values. No bound on the sum of `mask` on one device may be relied on, other than what follows from the above.
Results may differ from a plain program's by a relative error of at most 0.012.
The roundings to bfloat16 on the way count: a program that leaves them out, or rounds other values in their place, can miss the bound.
Values may be sent and summed in bfloat16 or wider, within the bound.
No kernel may reach another device: no remote copies, remote signals or barrier semaphores. Data moves between devices by JAX's collectives and lax.ppermute only.
A program may use at most 384 MiB of HBM per device.

v0:
```python
from functools import partial

import jax
import jax.numpy as jnp
from jax import lax
from jax.sharding import PartitionSpec as P

D = 1024
HEADS = 16
HEAD = 64
FF = 4096
V = 1024
ACTIONS = 8
NDOM = 4
BLOCK = 64
STEP = 10


highest = lax.Precision.HIGHEST
eps_norm = 1e-05
beta_first = 0.9
beta_second = 0.95
beta_stats = 0.95
rate_matrix = 0.2
rate_vector = 0.2
weight_decay = 0.01
eps_adam = 1e-08
masked_score = -1e30


def slab_widths():
    return [3 * D, D, 3 * D, D, FF, FF, V, V]


def slab_starts():
    starts = [0]
    for extent in slab_widths():
        starts.append(starts[-1] + extent)
    return starts


def layer_norm(inputs, gains, offset):
    center = inputs - jnp.mean(inputs, -1, keepdims=True)
    spread = jnp.mean(center * center, -1, keepdims=True)
    return center * lax.rsqrt(spread + eps_norm) * gains + offset


def norm_back(inputs, gains, offset, grad_out):
    unused, pullback = jax.vjp(layer_norm, inputs, gains, offset)
    return pullback(grad_out)


def product(former, latter):
    return jnp.dot(former, latter, preferred_element_type=jnp.float32)


def product_rows(former, latter):
    return lax.dot_general(
        former, latter, (((0,), (0,)), ((), ())), preferred_element_type=jnp.float32
    )


def product_cols(former, latter):
    return lax.dot_general(
        former, latter, (((1,), (1,)), ((), ())), preferred_element_type=jnp.float32
    )


def scores_of(queries, key_rows, causal):
    scores = (
        jnp.einsum("bqhe,bkhe->bhqk", queries, key_rows, preferred_element_type=jnp.float32) * 0.125
    )
    if causal:
        length = scores.shape[-1]
        allowed = jnp.arange(length)[:, None] >= jnp.arange(length)[None, :]
        scores = jnp.where(allowed, scores, masked_score)
    return scores


def attend(queries, key_rows, value_rows, causal):
    scores = scores_of(queries, key_rows, causal)
    largest = jnp.max(scores, -1, keepdims=True)
    powers = jnp.exp(scores - largest)
    totals = jnp.sum(powers, -1, keepdims=True)
    attn_prob = (powers / totals).astype(jnp.bfloat16)
    result = jnp.einsum(
        "bhqk,bkhe->bqhe", attn_prob, value_rows, preferred_element_type=jnp.float32
    )
    return (result.astype(jnp.bfloat16), largest + jnp.log(totals))


def score_grad(queries, key_rows, value_rows, log_total, grad_out, causal, row_delta=None):
    scores = scores_of(queries, key_rows, causal)
    attn_prob = jnp.exp(scores - log_total)
    grad_prob = jnp.einsum(
        "bqhe,bkhe->bhqk", grad_out, value_rows, preferred_element_type=jnp.float32
    )
    row_delta = jnp.sum(grad_prob * attn_prob, -1, keepdims=True)
    grad_score = (attn_prob * (grad_prob - row_delta)).astype(jnp.bfloat16)
    return (attn_prob, grad_score, row_delta)


def attend_back(queries, key_rows, value_rows, log_total, grad_out, causal):
    attn_prob, grad_score, unused = score_grad(
        queries, key_rows, value_rows, log_total, grad_out, causal
    )
    grad_query = (
        jnp.einsum("bhqk,bkhe->bqhe", grad_score, key_rows, preferred_element_type=jnp.float32)
        * 0.125
    )
    grad_key = (
        jnp.einsum("bhqk,bqhe->bkhe", grad_score, queries, preferred_element_type=jnp.float32)
        * 0.125
    )
    grad_value = jnp.einsum(
        "bhqk,bqhe->bkhe",
        attn_prob.astype(jnp.bfloat16),
        grad_out,
        preferred_element_type=jnp.float32,
    )
    return (grad_query, grad_key, grad_value)


def to_time(array, clip_count, frames, local):
    extent = array.shape[-1]
    return (
        array.reshape(clip_count, frames, local, extent)
        .swapaxes(1, 2)
        .reshape(clip_count * local, frames, extent)
    )


def from_time(array, clip_count, frames, local):
    extent = array.shape[-1]
    return (
        array.reshape(clip_count, local, frames, extent)
        .swapaxes(1, 2)
        .reshape(clip_count * frames * local, extent)
    )


def split_heads(array, groups):
    return array.reshape(array.shape[0], array.shape[1], groups, HEADS, HEAD)


def soap_update(weights, moment, second, stats, bases, grad):
    new_moment = beta_first * moment + (1.0 - beta_first) * grad
    first_fix = 1.0 - beta_first**STEP
    second_fix = 1.0 - beta_second**STEP
    starts = slab_starts()
    blocks = weights.shape[0] // BLOCK
    weight_list, second_list, stat_list, basis_list = ([], [], [], [])
    for number in range(8):
        begin = starts[number]
        finish = starts[number + 1]
        block_shape = (blocks, BLOCK, finish - begin)
        grad_block = grad[:, begin:finish].reshape(block_shape)
        moment_block = new_moment[:, begin:finish].reshape(block_shape)
        weight_block = weights[:, begin:finish].reshape(block_shape)
        basis = bases[number].reshape(blocks, BLOCK, BLOCK)
        stat = stats[number].reshape(blocks, BLOCK, BLOCK)
        grad_rot = jnp.einsum("bki,bkc->bic", basis, grad_block, precision=highest)
        moment_rot = jnp.einsum("bki,bkc->bic", basis, moment_block, precision=highest)
        second_new = (
            beta_second * second[:, begin:finish].reshape(block_shape)
            + (1.0 - beta_second) * grad_rot * grad_rot
        )
        direction = moment_rot / first_fix / (jnp.sqrt(second_new / second_fix) + eps_adam)
        stepped = jnp.einsum("bik,bkc->bic", basis, direction, precision=highest)
        weight_new = weight_block - rate_matrix * (stepped + weight_decay * weight_block)
        stat_new = beta_stats * stat + (1.0 - beta_stats) * jnp.einsum(
            "bic,bkc->bik", grad_block, grad_block, precision=highest
        )
        turned = jnp.einsum("bik,bkj->bij", stat_new, basis, precision=highest)
        gram = jnp.einsum("bki,bkj->bij", turned, turned, precision=highest)
        factor = jnp.linalg.cholesky(gram)
        basis_new = jnp.swapaxes(
            lax.linalg.triangular_solve(
                factor, jnp.swapaxes(turned, 1, 2), left_side=True, lower=True
            ),
            1,
            2,
        )
        weight_list.append(weight_new.reshape(blocks * BLOCK, finish - begin))
        second_list.append(second_new.reshape(blocks * BLOCK, finish - begin))
        stat_list.append(stat_new.reshape(blocks * BLOCK, BLOCK))
        basis_list.append(basis_new.reshape(blocks * BLOCK, BLOCK))
    return (
        jnp.concatenate(weight_list, 1),
        new_moment,
        jnp.concatenate(second_list, 1),
        jnp.stack(stat_list),
        jnp.stack(basis_list),
    )


def adam_update(values, moment, second, grad):
    new_moment = beta_first * moment + (1.0 - beta_first) * grad
    new_second = beta_second * second + (1.0 - beta_second) * grad * grad
    corrected = (
        new_moment
        / (1.0 - beta_first**STEP)
        / (jnp.sqrt(new_second / (1.0 - beta_second**STEP)) + eps_adam)
    )
    return (values - rate_vector * corrected, new_moment, new_second)


def body(
    codes,
    mask,
    actions,
    domains,
    weights,
    weight_m,
    weight_v,
    stats,
    bases,
    vectors,
    vector_m,
    vector_v,
):
    full, vec_low = (
        lax.all_gather(weights.astype(jnp.bfloat16), "clip", axis=0, tiled=True),
        lax.all_gather(vectors.astype(jnp.bfloat16), "clip", axis=1, tiled=True),
    )
    vecs = vec_low.astype(jnp.float32)
    starts = slab_starts()
    slabs = [full[:, starts[number] : starts[number + 1]] for number in range(8)]
    space_in, space_out, time_in, time_out, feed_up, feed_down, embed_table, head_table = slabs
    clip_count, frames, local = codes.shape
    frame_rows = clip_count * frames
    token_rows = frame_rows * local
    shape_args = (clip_count, frames, local)
    domain_hot = (domains[:, None] == jnp.arange(NDOM)[None, :]).astype(jnp.float32)
    masked_clip = jnp.sum(mask.astype(jnp.float32), axis=(1, 2))
    count_part = jnp.sum(domain_hot * masked_clip[:, None], 0)
    code_hot = (codes.reshape(token_rows)[:, None] == jnp.arange(V)[None, :]).astype(jnp.bfloat16)
    looked = product_cols(code_hot, embed_table)
    mask_col = mask.reshape(token_rows, 1).astype(jnp.float32)
    action_hot = (actions.reshape(frame_rows)[:, None] == jnp.arange(ACTIONS)[None, :]).astype(
        jnp.float32
    )
    action_add = jnp.dot(action_hot, vecs[9:], precision=highest)
    stream_zero = (
        mask_col * vecs[8] + (1.0 - mask_col) * looked + jnp.repeat(action_add, local, axis=0)
    )
    normed_s = layer_norm(stream_zero, vecs[0], vecs[4]).astype(jnp.bfloat16)
    projected_s = product(normed_s, space_in).astype(jnp.bfloat16).reshape(frame_rows, local, 3 * D)
    query_s = projected_s[:, :, :D].reshape(frame_rows, local, HEADS, HEAD)
    frame_kv = split_heads(lax.all_gather(projected_s[:, :, D:], "tile", axis=1, tiled=True), 2)
    keys_s = frame_kv[:, :, 0]
    values_s = frame_kv[:, :, 1]
    attended_s, log_s = attend(query_s, keys_s, values_s, False)
    attended_s = attended_s.reshape(token_rows, D)
    stream_one = stream_zero + product(attended_s, space_out)
    normed_t = layer_norm(stream_one, vecs[1], vecs[5]).astype(jnp.bfloat16)
    projected_t = split_heads(
        to_time(product(normed_t, time_in).astype(jnp.bfloat16), *shape_args), 3
    )
    query_t = projected_t[:, :, 0]
    keys_t = projected_t[:, :, 1]
    values_t = projected_t[:, :, 2]
    attended_t, log_t = attend(query_t, keys_t, values_t, True)
    attended_t = from_time(attended_t.reshape(clip_count * local, frames, D), *shape_args)
    stream_two = stream_one + product(attended_t, time_out)
    normed_f = layer_norm(stream_two, vecs[2], vecs[6]).astype(jnp.bfloat16)
    hidden_up = product(normed_f, feed_up)
    activated = jax.nn.gelu(hidden_up, approximate=False).astype(jnp.bfloat16)
    stream_three = stream_two + product_cols(activated, feed_down)
    normed_o = layer_norm(stream_three, vecs[3], vecs[7]).astype(jnp.bfloat16)
    logits = product(normed_o, head_table)
    largest = jnp.max(logits, -1, keepdims=True)
    log_sum = largest + jnp.log(jnp.sum(jnp.exp(logits - largest), -1, keepdims=True))
    code_float = code_hot.astype(jnp.float32)
    picked = jnp.sum(logits * code_float, -1, keepdims=True)
    token_loss = (log_sum - picked) * mask_col
    clip_total = jnp.sum(token_loss.reshape(clip_count, frames * local), 1)
    ce_part = jnp.sum(domain_hot * clip_total[:, None], 0)
    counts, ce_total = lax.psum((count_part, ce_part), ("clip", "tile"))
    inverse = 1.0 / jnp.maximum(counts, 1.0)
    clip_weight = jnp.sum(domain_hot * inverse[None, :], 1) / NDOM
    token_weight = jnp.repeat(clip_weight, frames * local)[:, None] * mask_col
    grad_logits = (token_weight * (jnp.exp(logits - log_sum) - code_float)).astype(jnp.bfloat16)
    grad_head = product_rows(normed_o, grad_logits)
    grad_stream, gain_o, offset_o = norm_back(
        stream_three, vecs[3], vecs[7], product_cols(grad_logits, head_table)
    )
    branch = grad_stream.astype(jnp.bfloat16)
    grad_down = product_rows(branch, activated)
    grad_act = product(branch, feed_down)
    unused, gelu_back = jax.vjp(partial(jax.nn.gelu, approximate=False), hidden_up)
    grad_up_rows = gelu_back(grad_act)[0].astype(jnp.bfloat16)
    grad_up = product_rows(normed_f, grad_up_rows)
    back_x, gain_f, offset_f = norm_back(
        stream_two, vecs[2], vecs[6], product_cols(grad_up_rows, feed_up)
    )
    grad_stream = grad_stream + back_x
    branch = grad_stream.astype(jnp.bfloat16)
    grad_time_out = product_rows(attended_t, branch)
    grad_mixed = to_time(product_cols(branch, time_out).astype(jnp.bfloat16), *shape_args)
    grad_mixed = grad_mixed.reshape(clip_count * local, frames, HEADS, HEAD)
    grad_query, grad_key, grad_value = attend_back(
        query_t, keys_t, values_t, log_t, grad_mixed, True
    )
    time_grad = jnp.concatenate(
        [
            piece.reshape(clip_count * local, frames, D)
            for piece in (grad_query, grad_key, grad_value)
        ],
        -1,
    )
    time_grad = from_time(time_grad, *shape_args).astype(jnp.bfloat16)
    grad_time_in = product_rows(normed_t, time_grad)
    back_x, gain_t, offset_t = norm_back(
        stream_one, vecs[1], vecs[5], product_cols(time_grad, time_in)
    )
    grad_stream = grad_stream + back_x
    branch = grad_stream.astype(jnp.bfloat16)
    grad_space_out = product_rows(attended_s, branch)
    grad_mixed = (
        product_cols(branch, space_out).astype(jnp.bfloat16).reshape(frame_rows, local, HEADS, HEAD)
    )
    grad_query, grad_key, grad_value = attend_back(
        query_s, keys_s, values_s, log_s, grad_mixed, False
    )
    frame_grad = jnp.concatenate(
        [grad_key.reshape(frame_rows, -1, D), grad_value.reshape(frame_rows, -1, D)], -1
    )
    own_kv = lax.psum_scatter(
        frame_grad.astype(jnp.bfloat16), "tile", scatter_dimension=1, tiled=True
    ).astype(jnp.float32)
    space_grad = jnp.concatenate([grad_query.reshape(frame_rows, local, D), own_kv], -1)
    space_grad = space_grad.reshape(token_rows, 3 * D).astype(jnp.bfloat16)
    grad_space_in = product_rows(normed_s, space_grad)
    back_x, gain_s, offset_s = norm_back(
        stream_zero, vecs[0], vecs[4], product_cols(space_grad, space_in)
    )
    grad_stream = grad_stream + back_x
    grad_embed = product_rows(((1.0 - mask_col) * grad_stream).astype(jnp.bfloat16), code_hot)
    grad_mask = jnp.sum(mask_col * grad_stream, 0)
    frame_sum = jnp.sum(grad_stream.reshape(frame_rows, local, D), 1)
    grad_action = jnp.dot(action_hot.T, frame_sum, precision=highest)
    grad_w = jnp.concatenate(
        [
            grad_space_in,
            grad_space_out,
            grad_time_in,
            grad_time_out,
            grad_up,
            grad_down,
            grad_embed,
            grad_head,
        ],
        1,
    )
    grad_v = jnp.concatenate(
        [
            jnp.stack(
                [gain_s, gain_t, gain_f, gain_o, offset_s, offset_t, offset_f, offset_o, grad_mask]
            ),
            grad_action,
        ],
        0,
    )
    owned_w, owned_v = (
        lax.psum_scatter(
            grad_w.astype(jnp.bfloat16), "clip", scatter_dimension=0, tiled=True
        ).astype(jnp.float32),
        lax.psum_scatter(
            grad_v.astype(jnp.bfloat16), "clip", scatter_dimension=1, tiled=True
        ).astype(jnp.float32),
    )
    owned_w, owned_v = (
        lax.psum(owned_w.astype(jnp.bfloat16), "tile").astype(jnp.float32),
        lax.psum(owned_v.astype(jnp.bfloat16), "tile").astype(jnp.float32),
    )
    tiles = lax.axis_size("tile")
    placed = lax.axis_index("tile")
    row_part = owned_w.shape[0] // tiles
    col_part = owned_v.shape[1] // tiles
    part_w = lax.dynamic_slice_in_dim(owned_w, placed * row_part, row_part, 0)
    part_v = lax.dynamic_slice_in_dim(owned_v, placed * col_part, col_part, 1)
    squares = jnp.sum(part_w * part_w) + jnp.sum(part_v * part_v)
    norm_sq = lax.psum(squares, ("clip", "tile"))
    grad_norm = jnp.sqrt(norm_sq)
    clip_scale = 1.0 / jnp.maximum(grad_norm, 1.0)
    new_weights, new_weight_m, new_weight_v, new_stats, new_bases = soap_update(
        weights, weight_m, weight_v, stats, bases, owned_w * clip_scale
    )
    new_vectors, new_vector_m, new_vector_v = adam_update(
        vectors, vector_m, vector_v, owned_v * clip_scale
    )
    loss_terms = jnp.stack([ce_total, counts])
    return (
        loss_terms,
        grad_norm,
        new_weights,
        new_weight_m,
        new_weight_v,
        new_stats,
        new_bases,
        new_vectors,
        new_vector_m,
        new_vector_v,
    )


def solution(mesh):
    placed = (
        P("clip", None, "tile"),
        P("clip", None, "tile"),
        P("clip", None),
        P("clip"),
        P("clip", None),
        P("clip", None),
        P("clip", None),
        P(None, "clip", None),
        P(None, "clip", None),
        P(None, "clip"),
        P(None, "clip"),
        P(None, "clip"),
    )
    return jax.shard_map(
        body,
        mesh=mesh,
        in_specs=placed,
        out_specs=(
            P(),
            P(),
            P("clip", None),
            P("clip", None),
            P("clip", None),
            P(None, "clip", None),
            P(None, "clip", None),
            P(None, "clip"),
            P(None, "clip"),
            P(None, "clip"),
        ),
        check_vma=False,
    )
```

profile of v0, /device:TPU:0, one launch (start us, length us, event | category | flops | bytes accessed | tf_op | source)
XLA Modules:
  0.0 2801.5 jit_solution(15400719086986040271)
XLA Ops:
  14.5 78.2 %all_gather.9 = bf16[17,1024]{1,0:T(8,128)(2,1)S(1)} all-gather(bf16[17,128]{1,0:T(8,128)(2,1)S(1)} %convert_element_type.141), channel_id=1, replica_groups=mesh['clip'=8,'tile'=4] {'clip'}, dimensions={1}, use_global_device_ids=true | all-gather | bytes 39168 | tf_op jit(solution)/shard_map/all_gather | solution.py:224
  93.5 640.2 %all-gather.3.cloned.1.call-done = bf16[1024,18432]{1,0:T(8,128)(2,1)} async-done(((bf16[128,18432]{1,0:T(8,128)(2,1)}), bf16[1024,18432]{1,0:T(8,128)(2,1)}) %all-gather.3.cloned.1.call-update) | async-done | bytes 37748752 | tf_op jit(solution)/shard_map/all_gather | solution.py:223
  740.1 10.0 convolution_convert_fusion.1
  763.5 99.7 %all-gather.5.cloned.1.call-done = bf16[16,256,2048]{2,0,1:T(8,128)(2,1)} async-done(((bf16[16,64,2048]{2,0,1:T(8,128)(2,1)}), bf16[16,256,2048]{2,0,1:T(8,128)(2,1)}) %all-gather.5.cloned.1.call-update) | async-done | bytes 16777232 | tf_op jit(solution)/shard_map/all_gather | solution.py:250
  863.1 23.7 copy.325
  886.9 12.9 multiply_reduce_fusion.1
  940.1 10.2 convolution_convert_fusion
  956.5 16.0 reshape_reshape.9
  1011.9 50.6 %multiply_convert_fusion.2 = (bf16[1024,4096]{1,0:T(8,128)(2,1)S(1)}, f32[1024,4096]{1,0:T(8,128)}, f32[1024,4096]{1,0:T(8,128)}) fusion(bf16[1024,18432]{1,0:T(8,128)(2,1)} %all-gather.3.cloned.1.call-done, f32[1024,1024]{1,0:T(8,128)S(1)} %get-tuple-element.134, f32[1024]{0:T(1024)S(1)} %bitcast.725, f32[1024]{0:T(1024)S(1)} %bitcast.711, ...), kind=kOutput, calls=%fused_computation.8 | convolution fusion | flops 8867807232 | bytes 54542336 | tf_op jit(solution)/shard_map/dot_general | solution.py:54
  1062.6 14.4 fusion.204
  1087.8 39.6 %psum.36 = f32[4]{0:T(128)S(1)} all-reduce(f32[4]{0:T(128)S(1)} %fusion.170), channel_id=1, replica_groups=mesh['clip'=8,'tile'=4] {'clip','tile'}, use_global_device_ids=true, to_apply=%region_18.19 | all-reduce | flops 4 | bytes 32 | tf_op jit(solution)/shard_map/psum | solution.py:279
  1140.6 23.7 add_convert_fusion
  1164.4 15.6 multiply_reduce_fusion.5
  1194.0 13.4 multiply_reduce_fusion.2
  1270.7 12.6 multiply_reduce_fusion.6
  1303.2 19.9 multiply_reduce_fusion
  1332.7 13.4 multiply_convert_fusion.1
  1346.1 10.9 multiply_convert_fusion
  1357.0 12.2 copy.349
  1369.3 12.2 copy.350
  1381.5 13.9 pad_maximum_fusion
  1395.5 10.6 fusion.54
  1440.2 82.3 %reduce-scatter.6.cloned.1.call-done = bf16[16,64,2048]{2,1,0:T(8,128)(2,1)} async-done(((bf16[16,256,2048]{2,1,0:T(8,128)(2,1)}), bf16[16,64,2048]{2,1,0:T(8,128)(2,1)}) %reduce-scatter.6.cloned.1.call-update) | async-done | bytes 4194320 | tf_op jit(solution)/shard_map/reduce_scatter | solution.py:329
  1522.5 13.1 convert_dynamic-update-slice_fusion.3
  1535.6 12.0 multiply_reduce_fusion.7
  1554.1 12.0 convert_dynamic-update-slice_fusion.2
  1569.0 15.6 convert_dynamic-update-slice_fusion.1
  1584.7 15.2 convert_dynamic-update-slice_fusion
  1628.6 587.9 %reduce-scatter.8.cloned.1.call-done = bf16[128,18432]{1,0:T(8,128)(2,1)} async-done(((bf16[1024,18432]{1,0:T(8,128)(2,1)}), bf16[128,18432]{1,0:T(8,128)(2,1)}) %reduce-scatter.8.cloned.1.call-update) | async-done | bytes 4718608 | tf_op jit(solution)/shard_map/reduce_scatter | solution.py:366
  2234.3 46.4 %reduce-scatter.10.cloned.1.call-done = bf16[128,17]{1,0:T(8,128)(2,1)} async-done(((bf16[1024,17]{1,0:T(8,128)(2,1)}), bf16[128,17]{1,0:T(8,128)(2,1)}) %reduce-scatter.10.cloned.1.call-update) | async-done | bytes 4368
  2288.0 88.0 %all-reduce.3.cloned.1.call-done = bf16[128,18432]{1,0:T(8,128)(2,1)} async-done(((bf16[128,18432]{1,0:T(8,128)(2,1)}), bf16[128,18432]{1,0:T(8,128)(2,1)}) %all-reduce.3.cloned.1.call-update) | async-done | bytes 4718608 | tf_op jit(solution)/shard_map/psum | solution.py:374
  2382.5 39.7 %all-reduce = (f32[1,4]{1,0:T(1,128)}, f32[]{:T(128)}) all-reduce(f32[1,4]{1,0:T(1,128)S(1)} %select_bitcast_fusion.8, f32[]{:T(128)S(6)} %add.311), channel_id=1, replica_groups=mesh['clip'=8,'tile'=4] {'clip','tile'}, use_global_device_ids=true, to_apply=%region_16.17 | all-reduce | flops 5 | bytes 40 | tf_op jit(solution)/shard_map/psum | solution.py:279
  2447.5 13.1 custom-call.20
  2468.3 13.1 custom-call.32
  2489.7 13.5 custom-call.30
  2512.9 13.1 custom-call.28
  2533.2 13.1 custom-call.26
  2555.3 13.1 custom-call.24
  2575.7 13.1 custom-call.22
  2596.4 13.2 custom-call.34
  2613.7 11.2 custom-call.35
  2628.3 11.2 custom-call.33
  2642.9 11.2 custom-call.31
  2657.5 11.2 custom-call.29
  2672.1 11.2 custom-call.27
  2686.7 11.2 custom-call.25
  2701.3 11.2 custom-call.23
  2715.9 11.4 custom-call.21
  (676 shorter events, 518.5 us)
Async XLA Ops:
  7.2 726.5 %all-gather.3.cloned.1.call-start = ((), (), s32[]{:S(2)}) async-start(), calls=%async_computation.3 | async-start | bytes 42467328 | tf_op jit(solution)/shard_map/all_gather | solution.py:223
  13.7 79.7 %copy-start.174 = (s32[1,16]{1,0:T(1,128)S(1)}, s32[1,16]{1,0:T(1,128)}, u32[]{:S(2)}) copy-start(s32[1,16]{1,0:T(1,128)} %param.17) | copy-start | bytes 196
  13.7 849.4 %all-gather.5.cloned.1.call-start = ((), (), s32[]{:S(2)}) async-start(), calls=%async_computation.4 | async-start | bytes 20971520 | tf_op jit(solution)/shard_map/all_gather | solution.py:250
  14.4 724.6 %copy-start.109 = (f32[1024]{0:T(1024)}, f32[1024]{0:T(1024)S(1)}, u32[]{:S(2)}) copy-start(f32[1024]{0:T(1024)S(1)} %convert_element_type.140) | copy-start | bytes 12292
  14.5 724.0 %copy-start.150 = (s32[1024]{0:T(1024)}, s32[1024]{0:T(1024)S(1)}, u32[]{:S(2)}) copy-start(s32[1024]{0:T(1024)S(1)} %eq.48) | copy-start | bytes 12292
  92.7 646.4 %copy-start.170 = (f32[1024]{0:T(1024)}, f32[1024]{0:T(1024)S(1)}, u32[]{:S(2)}) copy-start(f32[1024]{0:T(1024)S(1)} %broadcast_subtract_fusion) | copy-start | bytes 12292
  93.3 646.8 %copy-start.138 = (f32[1,1024]{1,0:T(1,128)}, f32[1,1024]{1,0:T(1,128)S(1)}, u32[]{:S(2)}) copy-start(f32[1,1024]{1,0:T(1,128)S(1)} %get-tuple-element.116) | copy-start | bytes 12292
  93.3 646.8 %copy-start.162 = (f32[1,1024]{1,0:T(1,128)}, f32[1,1024]{1,0:T(1,128)S(1)}, u32[]{:S(2)}) copy-start(f32[1,1024]{1,0:T(1,128)S(1)} %get-tuple-element.117) | copy-start | bytes 12292
  93.3 846.8 %copy-start.136 = (f32[1,1024]{1,0:T(1,128)}, f32[1,1024]{1,0:T(1,128)S(1)}, u32[]{:S(2)}) copy-start(f32[1,1024]{1,0:T(1,128)S(1)} %get-tuple-element.114) | copy-start | bytes 12292
  93.3 846.8 %copy-start.160 = (f32[1,1024]{1,0:T(1,128)}, f32[1,1024]{1,0:T(1,128)S(1)}, u32[]{:S(2)}) copy-start(f32[1,1024]{1,0:T(1,128)S(1)} %get-tuple-element.115) | copy-start | bytes 12292
  93.3 918.6 %copy-start.158 = (f32[1,1024]{1,0:T(1,128)}, f32[1,1024]{1,0:T(1,128)S(1)}, u32[]{:S(2)}) copy-start(f32[1,1024]{1,0:T(1,128)S(1)} %get-tuple-element.113) | copy-start | bytes 12292
  93.3 1086.7 %copy-start.134 = (f32[1,1024]{1,0:T(1,128)}, f32[1,1024]{1,0:T(1,128)S(1)}, u32[]{:S(2)}) copy-start(f32[1,1024]{1,0:T(1,128)S(1)} %get-tuple-element.112) | copy-start | bytes 12292
  757.2 765.3 %reduce-scatter.6.cloned.1.call-start = ((), (), s32[]{:S(2)}) async-start(), calls=%async_computation.5 | async-start | bytes 20971520 | tf_op jit(solution)/shard_map/reduce_scatter | solution.py:329
  758.3 232.2 %copy-start.130 = (pred[16,16]{0,1:T(8,128)(4,1)}, pred[16,16]{0,1:T(8,128)(4,1)S(1)}, u32[]{:S(2)}) copy-start(pred[16,16]{0,1:T(8,128)(4,1)S(1)} %iota_compare_fusion.6) | copy-start | bytes 772
  938.2 12.1 copy-start.9
  938.2 12.1 copy-start.116
  1011.3 51.2 %copy-start.16 = (f32[1024,1024]{1,0:T(8,128)}, f32[1024,1024]{1,0:T(8,128)S(1)}, u32[]{:S(2)}) copy-start(f32[1024,1024]{1,0:T(8,128)S(1)} %get-tuple-element.134) | copy-start | bytes 12582916
  1011.3 168.7 %copy-start.120 = (f32[1024]{0:T(1024)}, f32[1024]{0:T(1024)S(1)}, u32[]{:S(2)}) copy-start(f32[1024]{0:T(1024)S(1)} %broadcast_multiply_fusion.3) | copy-start | bytes 12292
  1011.9 50.6 %copy-start.126 = (f32[1024]{0:T(1024)}, f32[1024]{0:T(1024)S(1)}, u32[]{:S(2)}) copy-start(f32[1024]{0:T(1024)S(1)} %multiply_reduce_fusion.13) | copy-start | bytes 12292
  1011.9 168.1 %copy-start.146 = (f32[1024]{0:T(1024)}, f32[1024]{0:T(1024)S(1)}, u32[]{:S(2)}) copy-start(f32[1024]{0:T(1024)S(1)} %fusion.168) | copy-start | bytes 12292
  1062.5 14.5 copy-start.186
  1077.1 60.5 %copy-start.118 = (f32[1024]{0:T(1024)}, f32[1024]{0:T(1024)S(1)}, u32[]{:S(2)}) copy-start(f32[1024]{0:T(1024)S(1)} %broadcast_multiply_fusion.2) | copy-start | bytes 12292
  1077.6 60.0 %copy-start.144 = (f32[1024]{0:T(1024)}, f32[1024]{0:T(1024)S(1)}, u32[]{:S(2)}) copy-start(f32[1024]{0:T(1024)S(1)} %fusion.169) | copy-start | bytes 12292
  1083.0 45.6 %copy-start.110 = (f32[1024]{0:T(1024)S(1)}, f32[1024]{0:T(1024)}, u32[]{:S(2)}) copy-start(f32[1024]{0:T(1024)} %copy-done.109) | copy-start | bytes 12292
  1086.4 51.2 %copy-start.164 = (f32[1024]{0:T(1024)}, f32[1024]{0:T(1024)S(1)}, u32[]{:S(2)}) copy-start(f32[1024]{0:T(1024)S(1)} %get-tuple-element.52) | copy-start | bytes 12292
  1140.6 41.2 %copy-start.148 = (f32[1024]{0:T(1024)}, f32[1024]{0:T(1024)S(1)}, u32[]{:S(2)}) copy-start(f32[1024]{0:T(1024)S(1)} %negate_multiply_fusion.4) | copy-start | bytes 12292
  1140.6 23.7 copy-start.17
  1164.4 15.6 copy-start.127
  1270.7 12.7 copy-start.37
  1270.7 12.6 copy-start.125
  1303.2 19.9 copy-start.1
  1395.4 821.1 %reduce-scatter.8.cloned.1.call-start = ((), (), s32[]{:S(2)}) async-start(), calls=%async_computation.6 | async-start | bytes 42467328 | tf_op jit(solution)/shard_map/reduce_scatter | solution.py:366
  1437.2 85.2 %copy-start.115 = (f32[1024]{0:T(1024)S(1)}, f32[1024]{0:T(1024)}, u32[]{:S(2)}) copy-start(f32[1024]{0:T(1024)} %copy-done.114) | copy-start | bytes 12292
  1437.2 85.2 %copy-start.139 = (f32[1,1024]{1,0:T(1,128)S(1)}, f32[1,1024]{1,0:T(1,128)}, u32[]{:S(2)}) copy-start(f32[1,1024]{1,0:T(1,128)} %copy-done.138) | copy-start | bytes 12292
  1437.2 85.2 %copy-start.141 = (f32[1024]{0:T(1024)S(1)}, f32[1024]{0:T(1024)}, u32[]{:S(2)}) copy-start(f32[1024]{0:T(1024)} %copy-done.140) | copy-start | bytes 12292
  1437.2 85.2 %copy-start.163 = (f32[1,1024]{1,0:T(1,128)S(1)}, f32[1,1024]{1,0:T(1,128)}, u32[]{:S(2)}) copy-start(f32[1,1024]{1,0:T(1,128)} %copy-done.162) | copy-start | bytes 12292
  1522.4 13.1 copy-start.8
  1522.4 13.1 copy-start.46
  1522.5 13.1 copy-start.185
  1554.1 13.5 copy-start.121
  1554.1 13.5 copy-start.135
  1554.1 13.5 copy-start.147
  1554.1 13.5 copy-start.159
  1569.0 15.6 copy-start.20
  1569.0 15.6 copy-start.149
  1584.7 15.2 copy-start.25
  1611.1 669.6 %reduce-scatter.10.cloned.1.call-start = ((), (), s32[]{:S(2)}) async-start(), calls=%async_computation.8 | async-start | bytes 294912
  1628.5 747.5 %all-reduce.3.cloned.1.call-start = ((), (), s32[]{:S(2)}) async-start(), calls=%async_computation.7 | async-start | bytes 9437184 | tf_op jit(solution)/shard_map/psum | solution.py:374
  (147 other events, 526.2 us)
Sparse Core Ops, SparseCore 0:
  13.8 719.8 all-gather.2
  757.3 105.7 all-gather.4
  1395.5 126.8 reduce-scatter.5
  1611.2 605.1 reduce-scatter.7
  2220.2 60.4 reduce-scatter.9
  2282.9 93.0 all-reduce.2
where the time goes:
time: 2820 us; the launch traced here: 2800 us
  waiting for transfers between devices  1540 us (55%)
  matrix products  453 us (16%)
  other arithmetic  313 us (11%)
  local copies, waits for them, and re-layouts  306 us (11%)
  blocking collectives  163 us (6%)
    all_gather x1, waiting for transfers between devices, body(): lax.all_gather(weights.astype(jnp.bfloat16), 'clip', axis=0, tiled=True)  640 us
    reduce_scatter x1, waiting for transfers between devices, body(): lax.psum_scatter(grad_w.astype(jnp.bfloat16), 'clip', scatter_dimension=0...  588 us
    dot_general x7, matrix products, product(): return jnp.dot(former, latter, preferred_element_type=jnp.float32)  110 us
    another operation x18, other arithmetic, soap_update(): factor = jnp.linalg.cholesky(gram)  107 us
    all_gather x1, waiting for transfers between devices, body(): lax.all_gather(projected_s[:, :, D:], 'tile', axis=1, tiled=True)  99.7 us
    another operation x10, other arithmetic, soap_update(): lax.linalg.triangular_solve(factor, jnp.swapaxes(turned, 1, 2), left_side...  92.3 us
    psum x1, waiting for transfers between devices, body(): lax.psum(owned_w.astype(jnp.bfloat16), 'tile').astype(jnp.float32)  88 us
    reduce_scatter x1, waiting for transfers between devices, body(): lax.psum_scatter(frame_grad.astype(jnp.bfloat16), 'tile', scatter_dimensi...  82.3 us
  transfers between devices with their start and end apart: 6, of which 6 were waited for; matrix products, arithmetic and copies ran while one was open for 3% of the time, Pallas kernels for 0%

commit v1 on v0

v1 whole, which is shorter than its diff:
```python
from functools import partial

import jax
import jax.numpy as jnp
from jax import lax
from jax.experimental import pallas as pl
from jax.experimental.pallas import tpu as pltpu
from jax.sharding import PartitionSpec as P

D = 1024
HEADS = 16
HEAD = 64
FF = 4096
V = 1024
ACTIONS = 8
NDOM = 4
BLOCK = 64
STEP = 10
CORES = 2
LANES = 128
QUAD = 256
FOLD = 4


highest = lax.Precision.HIGHEST
eps_norm = 1e-05
beta_first = 0.9
beta_second = 0.95
beta_stats = 0.95
rate_matrix = 0.2
rate_vector = 0.2
weight_decay = 0.01
eps_adam = 1e-08
masked_score = -1e30
first_fix = 1.0 - beta_first**STEP
second_fix = 1.0 - beta_second**STEP

f32 = jnp.float32
bf16 = jnp.bfloat16

WIDTHS = [3 * D, D, 3 * D, D, FF, FF, V, V]
STARTS = [sum(WIDTHS[:number]) for number in range(9)]


def dot_nn(former, latter):
    return jnp.dot(former, latter, preferred_element_type=f32)


def dot_tn(former, latter):
    return lax.dot_general(former, latter, (((0,), (0,)), ((), ())), preferred_element_type=f32)


def dot_nt(former, latter):
    return lax.dot_general(former, latter, (((1,), (1,)), ((), ())), preferred_element_type=f32)


def norm_stats(inputs):
    mean = jnp.mean(inputs, -1, keepdims=True)
    center = inputs - mean
    spread = jnp.mean(center * center, -1, keepdims=True)
    return (mean, lax.rsqrt(spread + eps_norm))


def norm_apply(inputs, stat, gain, offset):
    mean, scale = stat
    return ((inputs - mean) * scale * gain + offset).astype(bf16)


def norm_back(inputs, stat, gain, grad_out):
    mean, scale = stat
    normal = (inputs - mean) * scale
    grad_gain = jnp.sum(grad_out * normal, 0)
    grad_offset = jnp.sum(grad_out, 0)
    error = grad_out * gain
    first = jnp.mean(error, -1, keepdims=True)
    second = jnp.mean(error * normal, -1, keepdims=True)
    return ((error - first - normal * second) * scale, grad_gain, grad_offset)


def gelu_pair(value):
    size = jnp.abs(value) * (0.5**0.5)
    ratio = 1.0 / (1.0 + 0.3275911 * size)
    bell = jnp.exp(-size * size)
    series = 1.061405429
    for term in (-1.453152027, 1.421413741, -0.284496736, 0.254829592):
        series = series * ratio + term
    tail = 0.5 * series * ratio * bell
    phi = jnp.where(value >= 0.0, 1.0 - tail, tail)
    return (value * phi, phi + value * bell * 0.3989422804014327)


def head_masks(rows):
    lane = lax.broadcasted_iota(jnp.int32, (rows, QUAD), 1) // HEAD
    return [lane == number for number in range(FOLD)]


def fold_heads(block):
    masks = head_masks(block.shape[0])
    zero = jnp.zeros_like(block)
    return jnp.concatenate([jnp.where(mask, block, zero) for mask in masks], 0)


def unfold_heads(stacked):
    rows = stacked.shape[0] // FOLD
    masks = head_masks(rows)
    total = jnp.where(masks[0], stacked[:rows], 0.0)
    for number in range(1, FOLD):
        total = jnp.where(masks[number], stacked[number * rows : (number + 1) * rows], total)
    return total


def allow_mask(shape, span, query_axis):
    query = lax.broadcasted_iota(jnp.int32, shape, query_axis)
    key = lax.broadcasted_iota(jnp.int32, shape, 1 - query_axis)
    if query_axis == 0:
        query = query % QUAD
    else:
        key = key % QUAD
    return (query % span == key % span) & (key // span <= query // span)


def attend_kernel(query_ref, key_ref, value_ref, out_ref, *, span):
    query = query_ref[...].reshape(QUAD, QUAD)
    key = key_ref[...].reshape(QUAD, QUAD)
    value = value_ref[...].reshape(QUAD, QUAD)
    scores = dot_nt(fold_heads(query), key) * 0.125
    if span:
        scores = jnp.where(allow_mask(scores.shape, span, 0), scores, masked_score)
    powers = jnp.exp(scores - jnp.max(scores, -1, keepdims=True))
    attn = (powers * (1.0 / jnp.sum(powers, -1, keepdims=True))).astype(bf16)
    mixed = unfold_heads(dot_nn(attn, value))
    out_ref[...] = mixed.astype(bf16).reshape(out_ref.shape)


def attend_back_kernel(
    query_ref, key_ref, value_ref, grad_ref, dquery_ref, dkey_ref, dvalue_ref, *, span
):
    query = query_ref[...].reshape(QUAD, QUAD)
    key = key_ref[...].reshape(QUAD, QUAD)
    value = value_ref[...].reshape(QUAD, QUAD)
    grad = grad_ref[...].reshape(QUAD, QUAD)
    key_fold = fold_heads(key)
    scores = dot_nt(key_fold, query) * 0.125
    if span:
        scores = jnp.where(allow_mask(scores.shape, span, 1), scores, masked_score)
    scores = scores.reshape(FOLD, QUAD, QUAD)
    powers = jnp.exp(scores - jnp.max(scores, 1, keepdims=True))
    attn = powers * (1.0 / jnp.sum(powers, 1, keepdims=True))
    grad_attn = dot_nt(fold_heads(value), grad).reshape(FOLD, QUAD, QUAD)
    delta = jnp.sum(grad_attn * attn, 1, keepdims=True)
    grad_score = (attn * (grad_attn - delta)).astype(bf16).reshape(FOLD * QUAD, QUAD)
    attn = attn.astype(bf16).reshape(FOLD * QUAD, QUAD)
    dvalue = unfold_heads(dot_nn(attn, grad))
    dkey = unfold_heads(dot_nn(grad_score, query)) * 0.125
    dquery = dot_tn(grad_score, key_fold) * 0.125
    dquery_ref[...] = dquery.astype(bf16).reshape(dquery_ref.shape)
    dkey_ref[...] = dkey.astype(bf16).reshape(dkey_ref.shape)
    dvalue_ref[...] = dvalue.astype(bf16).reshape(dvalue_ref.shape)


def attend_params():
    return pltpu.CompilerParams(
        vmem_limit_bytes=40 * 1024 * 1024, dimension_semantics=("arbitrary", "arbitrary")
    )


QUADS = D // QUAD


def space_spec(part):
    return pl.BlockSpec((QUAD, QUAD), lambda frame, quad, part=part: (frame, part * QUADS + quad))


def time_spec(part, span, frames):
    return pl.BlockSpec(
        (frames, span, QUAD), lambda group, quad, part=part: (0, group, part * QUADS + quad)
    )


def attend_space(projected):
    rows = projected.shape[0]
    return pl.pallas_call(
        partial(attend_kernel, span=0),
        grid=(rows // QUAD, QUADS),
        in_specs=[space_spec(0), space_spec(1), space_spec(2)],
        out_specs=space_spec(0),
        out_shape=jax.ShapeDtypeStruct((rows, D), bf16),
        compiler_params=attend_params(),
    )(projected, projected, projected)


def attend_space_back(projected, grad):
    rows = projected.shape[0]
    shape = jax.ShapeDtypeStruct((rows, D), bf16)
    parts = pl.pallas_call(
        partial(attend_back_kernel, span=0),
        grid=(rows // QUAD, QUADS),
        in_specs=[space_spec(0), space_spec(1), space_spec(2), space_spec(0)],
        out_specs=[space_spec(0)] * 3,
        out_shape=[shape] * 3,
        compiler_params=attend_params(),
    )(projected, projected, projected, grad)
    return jnp.concatenate(parts, -1)


def attend_time(projected, frames):
    rows = projected.shape[0]
    local = rows // frames
    span = QUAD // frames
    cube = projected.reshape(frames, local, 3 * D)
    return pl.pallas_call(
        partial(attend_kernel, span=span),
        grid=(local // span, QUADS),
        in_specs=[time_spec(part, span, frames) for part in range(3)],
        out_specs=time_spec(0, span, frames),
        out_shape=jax.ShapeDtypeStruct((frames, local, D), bf16),
        compiler_params=attend_params(),
    )(cube, cube, cube).reshape(rows, D)


def attend_time_back(projected, grad, frames):
    rows = projected.shape[0]
    local = rows // frames
    span = QUAD // frames
    cube = projected.reshape(frames, local, 3 * D)
    shape = jax.ShapeDtypeStruct((frames, local, D), bf16)
    parts = pl.pallas_call(
        partial(attend_back_kernel, span=span),
        grid=(local // span, QUADS),
        in_specs=[time_spec(part, span, frames) for part in range(3)]
        + [time_spec(0, span, frames)],
        out_specs=[time_spec(0, span, frames)] * 3,
        out_shape=[shape] * 3,
        compiler_params=attend_params(),
    )(cube, cube, cube, grad.reshape(frames, local, D))
    return jnp.concatenate([part.reshape(rows, D) for part in parts], -1)


class Level:
    def __init__(self, size, stride, total):
        self.size, self.stride, self.total = size, stride, total

    def digit(self):
        return (lax.axis_index(("clip", "tile")) // self.stride) % self.size

    def shift(self, array, step):
        pairs = []
        for source in range(self.total):
            digit = (source // self.stride) % self.size
            target = source + ((digit + step) % self.size - digit) * self.stride
            pairs.append((source, target))
        return lax.ppermute(array, ("clip", "tile"), pairs)

    def swap(self, array, flip):
        pairs = []
        for source in range(self.total):
            digit = (source // self.stride) % self.size
            pairs.append((source, source + ((digit ^ flip) - digit) * self.stride))
        return lax.ppermute(array, ("clip", "tile"), pairs)

    def sum(self, array):
        flip = 1
        while flip < self.size:
            array = array + self.swap(array, flip)
            flip *= 2
        return array


def make_levels(clips, tiles):
    total = clips * tiles
    across = tiles // CORES
    outer = 4 if clips % 4 == 0 else clips
    inner = clips // outer
    return {
        "core": Level(CORES, 1, total),
        "x": Level(across, CORES, total),
        "inner": Level(inner, tiles, total),
        "outer": Level(outer, tiles * inner, total),
    }


def cut(array, index, size, axis):
    return lax.dynamic_slice_in_dim(array, index * size, size, axis)


def assemble(level, pieces, axis):
    digit = level.digit()
    width = pieces[0].shape[axis]
    shape = list(pieces[0].shape)
    shape[axis] = width * level.size
    whole = jnp.zeros(shape, pieces[0].dtype)
    for step, piece in enumerate(pieces):
        place = (digit - step) % level.size
        whole = lax.dynamic_update_slice_in_dim(whole, piece, place * width, axis)
    return whole


def gather(level, piece, axis):
    pieces = [piece] + [level.shift(piece, step) for step in range(1, level.size)]
    return assemble(level, pieces, axis)


class Reducer:
    def __init__(self, levels):
        self.levels = levels
        self.core = levels["core"].digit()
        self.x = levels["x"].digit()
        self.inner = levels["inner"].digit()
        self.outer = levels["outer"].digit()

    def rows_of(self, former, inner):
        outer = self.levels["outer"].size
        count = self.levels["inner"].size
        rows = former.shape[-1] // (outer * count)
        split = former.reshape(former.shape[0], outer, count, rows)
        return lax.dynamic_index_in_dim(split, inner, 2, keepdims=False).reshape(
            former.shape[0], outer * rows
        )

    def row_cut(self, array, inner):
        outer = self.levels["outer"].size
        count = self.levels["inner"].size
        rows = array.shape[0] // (outer * count)
        split = array.reshape(outer, count, rows, array.shape[1])
        return lax.dynamic_index_in_dim(split, inner, 1, keepdims=False).reshape(
            outer * rows, array.shape[1]
        )

    def start(self, former, latter):
        width = latter.shape[1]
        across = self.levels["x"].size
        half, quarter = width // CORES, width // (CORES * across)
        other = cut(latter, 1 - self.core, half, 1)
        own = cut(latter, self.core, half, 1)
        from_core = self.levels["core"].shift(dot_tn(former, other).astype(bf16), 1)
        from_x = []
        for step in range(1, across):
            place = (self.x + step) % across
            part = dot_tn(former, cut(own, place, quarter, 1))
            part = part + cut(from_core, place, quarter, 1).astype(f32)
            from_x.append(self.levels["x"].shift(part.astype(bf16), step))
        kept = cut(own, self.x, quarter, 1)
        kept_core = cut(from_core, self.x, quarter, 1)

        def rows(inner):
            part = dot_tn(self.rows_of(former, inner), kept)
            for piece in [kept_core] + from_x:
                part = part + self.row_cut(piece, inner).astype(f32)
            return part

        return (quarter, rows)

    def start_vector(self, array):
        total = array
        for name in ("core", "x"):
            sent = total.astype(bf16)
            for step in range(1, self.levels[name].size):
                total = total + self.levels[name].shift(sent, step).astype(f32)

        def rows(inner):
            return self.row_cut(total, inner)

        return (array.shape[1], rows)

    def finish(self, started):
        inner, outer = self.levels["inner"], self.levels["outer"]
        from_inner = []
        for step in range(1, inner.size):
            place = (self.inner + step) % inner.size
            sent = jnp.concatenate([rows(place).astype(bf16) for _, rows in started], 1)
            from_inner.append(inner.shift(sent, step))
        total = jnp.concatenate([rows(self.inner) for _, rows in started], 1)
        for piece in from_inner:
            total = total + piece.astype(f32)
        count = total.shape[0] // outer.size
        low = total.astype(bf16)
        from_outer = []
        for step in range(1, outer.size):
            place = (self.outer + step) % outer.size
            from_outer.append(outer.shift(cut(low, place, count, 0), step))
        total = cut(total, self.outer, count, 0)
        for piece in from_outer:
            total = total + piece.astype(f32)
        return total

    def spread(self, quarters, sizes):
        low = quarters.astype(bf16)
        rows = low.shape[0]
        x, core = self.levels["x"], self.levels["core"]
        from_x = [low] + [x.shift(low, step) for step in range(1, x.size)]
        halves, begin = [], 0
        for size in sizes:
            halves.append(assemble(x, [piece[:, begin : begin + size] for piece in from_x], 1))
            begin += size
        half = jnp.concatenate(halves, 1)
        from_core = [half, core.shift(half, 1)]
        wholes, begin = [], 0
        for size in sizes:
            size = size * x.size
            wholes.append(assemble(core, [piece[:, begin : begin + size] for piece in from_core], 1))
            begin += size
        return wholes


def split_two(array):
    high = array.astype(bf16)
    return (high, (array - high.astype(f32)).astype(bf16))


def dot_three(left, right):
    return (
        dot_nn(left[0], right[0]) + dot_nn(left[1], right[0]) + dot_nn(left[0], right[1])
    )


def update_kernel(
    scale_ref, grad_ref, weight_ref, moment_ref, second_ref,
    turn_high_ref, turn_low_ref, back_high_ref, back_low_ref,
    new_weight_ref, new_moment_ref, new_second_ref,
):
    scale = scale_ref[0]
    grad = grad_ref[...]
    turn = (turn_high_ref[0], turn_low_ref[0])
    back = (back_high_ref[0], back_low_ref[0])
    moment = moment_ref[...]
    weight = weight_ref[...]
    grad_rot = (dot_nn(turn[0], grad) + dot_nn(turn[1], grad)) * scale
    new_moment_ref[...] = beta_first * moment + (1.0 - beta_first) * (grad.astype(f32) * scale)
    moment_rot = beta_first * dot_three(turn, split_two(moment)) + (1.0 - beta_first) * grad_rot
    second = beta_second * second_ref[...] + (1.0 - beta_second) * grad_rot * grad_rot
    new_second_ref[...] = second
    direction = (moment_rot * (1.0 / first_fix)) / (jnp.sqrt(second * (1.0 / second_fix)) + eps_adam)
    stepped = dot_three(back, split_two(direction))
    new_weight_ref[...] = weight - rate_matrix * (stepped + weight_decay * weight)


def matrix_of(chunk, size):
    number = 0
    for start in STARTS[1:8]:
        number = number + jnp.where(chunk * size >= start, 1, 0)
    return number


def update_weights(scale, grad, weights, moment, second, bases):
    rows, cols = weights.shape
    chunk = 1024
    blocks = rows // BLOCK
    square = bases.reshape(8, blocks, BLOCK, BLOCK)
    pick = jnp.eye(blocks, dtype=f32)
    wide = (square[:, :, :, None, :] * pick[None, :, None, :, None]).reshape(8, rows, rows)
    back = split_two(wide)
    turn = split_two(jnp.swapaxes(wide, 1, 2))
    slab = pl.BlockSpec((rows, chunk), lambda place: (0, place))
    basis = pl.BlockSpec((1, rows, rows), lambda place: (matrix_of(place, chunk), 0, 0))
    shape = jax.ShapeDtypeStruct((rows, cols), f32)
    return pl.pallas_call(
        update_kernel,
        grid=(cols // chunk,),
        in_specs=[pl.BlockSpec(memory_space=pltpu.SMEM)] + [slab] * 4 + [basis] * 4,
        out_specs=[slab] * 3,
        out_shape=[shape] * 3,
        compiler_params=pltpu.CompilerParams(
            vmem_limit_bytes=48 * 1024 * 1024, dimension_semantics=("arbitrary",)
        ),
    )(scale.reshape(1), grad, weights, moment, second, *turn, *back)


def dot_exact(former, latter, dims):
    return lax.dot_general(
        former, latter, (dims, ((), ())), precision=highest, preferred_element_type=f32
    )


def turn_kernel(scale_ref, outer_ref, stat_ref, basis_ref, new_stat_ref, new_basis_ref, work_ref):
    count = stat_ref.shape[0]
    scale = scale_ref[0]
    for number in range(count):
        stat = beta_stats * stat_ref[number] + (1.0 - beta_stats) * (
            scale * scale * outer_ref[number]
        )
        new_stat_ref[number] = stat
        turned = dot_exact(basis_ref[number], stat, ((0,), (1,)))
        gram = dot_exact(turned, turned, ((1,), (1,)))
        work_ref[number] = jnp.concatenate([gram, turned], 1)

    for stage in range(4):
        low = stage * (BLOCK // 4)
        shape = (count, BLOCK - low, 2 * BLOCK)
        lane = lax.broadcasted_iota(jnp.int32, shape, 2)
        line = lax.broadcasted_iota(jnp.int32, shape, 1) + low

        def step(place, carry, low=low, lane=lane, line=line):
            held = work_ref[:, low:, :]
            row = jnp.sum(jnp.where(line == place, held, 0.0), 1, keepdims=True)
            column = jnp.sum(jnp.where(lane == place, held, 0.0), 2, keepdims=True)
            pivot = jnp.sum(jnp.where(lane[:, :1] == place, row, 0.0), 2, keepdims=True)
            inverse = lax.rsqrt(pivot)
            row = row * inverse
            column = column * inverse
            done = held - column * row
            held = jnp.where(line > place, done, held)
            work_ref[:, low:, :] = jnp.where(line == place, row, held)
            return carry

        lax.fori_loop(low, low + BLOCK // 4, step, 0)

    for number in range(count):
        new_basis_ref[number] = jnp.transpose(work_ref[number])[BLOCK:, :]


def turn_bases(scale, outers, stats, bases):
    rows = stats.shape[1]
    count = 8 * rows // BLOCK
    cubes = [array.reshape(count, BLOCK, BLOCK) for array in (outers, stats, bases)]
    shape = jax.ShapeDtypeStruct((count, BLOCK, BLOCK), f32)
    new_stats, new_bases = pl.pallas_call(
        turn_kernel,
        in_specs=[pl.BlockSpec(memory_space=pltpu.SMEM)]
        + [pl.BlockSpec(memory_space=pltpu.VMEM)] * 3,
        out_specs=[pl.BlockSpec(memory_space=pltpu.VMEM)] * 2,
        out_shape=[shape] * 2,
        scratch_shapes=[pltpu.VMEM((count, BLOCK, 2 * BLOCK), f32)],
        compiler_params=pltpu.CompilerParams(vmem_limit_bytes=32 * 1024 * 1024),
    )(scale.reshape(1), *cubes)
    return (new_stats.reshape(8, rows, BLOCK), new_bases.reshape(8, rows, BLOCK))


def adam_update(values, moment, second, grad):
    new_moment = beta_first * moment + (1.0 - beta_first) * grad
    new_second = beta_second * second + (1.0 - beta_second) * grad * grad
    corrected = (
        new_moment
        / (1.0 - beta_first**STEP)
        / (jnp.sqrt(new_second / (1.0 - beta_second**STEP)) + eps_adam)
    )
    return (values - rate_vector * corrected, new_moment, new_second)


def body(
    sizes,
    codes,
    mask,
    actions,
    domains,
    weights,
    weight_m,
    weight_v,
    stats,
    bases,
    vectors,
    vector_m,
    vector_v,
):
    clips, tiles = sizes
    levels = make_levels(clips, tiles)
    tile = lax.axis_index("tile")
    unused, frames, local = codes.shape
    own_frames = frames // tiles
    positions = local * tiles
    both = ("clip", "tile")

    vec_rows = vectors.shape[1] // tiles
    vec_own = cut(vectors, tile, vec_rows, 1).T.astype(bf16)
    vec_own = jnp.pad(vec_own, ((0, 0), (0, LANES - vec_own.shape[1])))
    row_part = weights.shape[0] // tiles
    part = cut(weights, tile, row_part, 0).astype(bf16)

    def slab(number):
        return part[:, STARTS[number] : STARTS[number + 1]]

    def fetch(pieces):
        whole = lax.all_gather(jnp.concatenate(pieces, 1), both, axis=0, tiled=True)
        parts, begin = [], 0
        for piece in pieces:
            parts.append(whole[:, begin : begin + piece.shape[1]])
            begin += piece.shape[1]
        return parts

    embed_table, space_in, vec_cols = fetch([slab(6), slab(0), vec_own])
    space_out, time_in, time_out = fetch([slab(1), slab(2), slab(3)])
    feed_up, feed_down, head_table = fetch([slab(4), slab(5), slab(7)])
    vecs = vec_cols[:, : vectors.shape[0]].T.astype(f32)

    domain_hot = (domains[:, None] == jnp.arange(NDOM)[None, :]).astype(f32)
    masked_clip = jnp.sum(mask.astype(f32), axis=(1, 2))
    counts = jnp.sum(domain_hot * masked_clip[:, None], 0)
    for name in ("core", "x", "inner", "outer"):
        counts = levels[name].sum(counts)
    inverse = 1.0 / jnp.maximum(counts, 1.0)
    clip_weight = jnp.sum(domain_hot * inverse[None, :]) / NDOM

    packed = lax.all_gather(codes[0] + V * mask[0], "tile", axis=1, tiled=True)
    packed = cut(packed, tile, own_frames, 0)
    frame_codes, frame_mask = packed % V, packed // V
    action_hot = (actions[0][:, None] == jnp.arange(ACTIONS)[None, :]).astype(f32)
    action_add = jnp.dot(action_hot, vecs[9:], precision=highest)

    def embed(code, masked, action_rows, span):
        rows = code.size
        hot = (code.reshape(rows)[:, None] == jnp.arange(V)[None, :]).astype(bf16)
        masked = masked.reshape(rows, 1).astype(f32)
        looked = dot_nt(hot, embed_table)
        added = jnp.repeat(action_rows, span, axis=0)
        return (hot, masked, masked * vecs[8] + (1.0 - masked) * looked + added)

    frame_hot, frame_col, frame_zero = embed(
        frame_codes, frame_mask, cut(action_add, tile, own_frames, 0), positions
    )
    code_hot, mask_col, stream_zero = embed(codes[0], mask[0], action_add, local)

    stat_s = norm_stats(frame_zero)
    normed_s = norm_apply(frame_zero, stat_s, vecs[0], vecs[4])
    projected_s = dot_nn(normed_s, space_in).astype(bf16)
    mixed_s = attend_space(projected_s)

    def flip(array, step):
        pairs = [(source, (source + step) % tiles) for source in range(tiles)]
        return lax.ppermute(array, "tile", pairs)

    def to_positions(array):
        cube = array.reshape(own_frames, tiles, local, D).swapaxes(0, 1)
        whole = jnp.zeros((tiles, own_frames, local, D), bf16)
        for step in range(tiles):
            piece = lax.dynamic_index_in_dim(cube, (tile + step) % tiles, 0)
            if step:
                piece = flip(piece, step)
            whole = lax.dynamic_update_slice_in_dim(whole, piece, (tile - step) % tiles, 0)
        return whole.reshape(frames * local, D)

    def to_frames(array):
        cube = array.reshape(tiles, own_frames, local, D)
        whole = jnp.zeros((tiles, own_frames, local, D), bf16)
        for step in range(tiles):
            piece = lax.dynamic_index_in_dim(cube, (tile + step) % tiles, 0)
            if step:
                piece = flip(piece, step)
            whole = lax.dynamic_update_slice_in_dim(whole, piece, (tile - step) % tiles, 0)
        return whole.swapaxes(0, 1).reshape(own_frames * positions, D)

    attended_s = to_positions(mixed_s)
    stream_one = stream_zero + dot_nn(attended_s, space_out)

    stat_t = norm_stats(stream_one)
    normed_t = norm_apply(stream_one, stat_t, vecs[1], vecs[5])
    projected_t = dot_nn(normed_t, time_in).astype(bf16)
    attended_t = attend_time(projected_t, frames)
    stream_two = stream_one + dot_nn(attended_t, time_out)

    stat_f = norm_stats(stream_two)
    normed_f = norm_apply(stream_two, stat_f, vecs[2], vecs[6])
    activated, slope = gelu_pair(dot_nn(normed_f, feed_up))
    activated = activated.astype(bf16)
    stream_three = stream_two + dot_nt(activated, feed_down)

    stat_o = norm_stats(stream_three)
    normed_o = norm_apply(stream_three, stat_o, vecs[3], vecs[7])
    logits = dot_nn(normed_o, head_table)
    largest = jnp.max(logits, -1, keepdims=True)
    log_sum = largest + jnp.log(jnp.sum(jnp.exp(logits - largest), -1, keepdims=True))
    code_float = code_hot.astype(f32)
    picked = jnp.sum(logits * code_float, -1, keepdims=True)
    ce_part = domain_hot[0] * jnp.sum((log_sum - picked) * mask_col)
    token_weight = clip_weight * mask_col
    grad_logits = (token_weight * (jnp.exp(logits - log_sum) - code_float)).astype(bf16)

    reducer = Reducer(levels)
    head_part = reducer.start(normed_o, grad_logits)
    grad_stream, gain_o, offset_o = norm_back(
        stream_three, stat_o, vecs[3], dot_nt(grad_logits, head_table)
    )
    branch = grad_stream.astype(bf16)
    down_part = reducer.start(branch, activated)
    grad_up_rows = (dot_nn(branch, feed_down) * slope).astype(bf16)
    up_part = reducer.start(normed_f, grad_up_rows)
    back_x, gain_f, offset_f = norm_back(stream_two, stat_f, vecs[2], dot_nt(grad_up_rows, feed_up))
    grad_stream = grad_stream + back_x
    branch = grad_stream.astype(bf16)
    time_out_part = reducer.start(attended_t, branch)
    grad_mixed = dot_nt(branch, time_out).astype(bf16)
    time_grad = attend_time_back(projected_t, grad_mixed, frames)
    time_in_part = reducer.start(normed_t, time_grad)
    back_x, gain_t, offset_t = norm_back(stream_one, stat_t, vecs[1], dot_nt(time_grad, time_in))
    grad_stream = grad_stream + back_x
    branch = grad_stream.astype(bf16)
    grad_mixed = to_frames(dot_nt(branch, space_out).astype(bf16))
    space_out_part = reducer.start(attended_s, branch)
    space_grad = attend_space_back(projected_s, grad_mixed)
    space_in_part = reducer.start(normed_s, space_grad)
    back_x, gain_s, offset_s = norm_back(frame_zero, stat_s, vecs[0], dot_nt(space_grad, space_in))

    embed_former = jnp.concatenate([(1.0 - mask_col) * grad_stream, (1.0 - frame_col) * back_x], 0)
    embed_part = reducer.start(
        embed_former.astype(bf16), jnp.concatenate([code_hot, frame_hot], 0)
    )
    grad_mask = jnp.sum(mask_col * grad_stream, 0) + jnp.sum(frame_col * back_x, 0)
    frame_sum = jnp.sum(grad_stream.reshape(frames, local, D), 1)
    own_sum = jnp.sum(back_x.reshape(own_frames, positions, D), 1)
    own_hot = cut(action_hot, tile, own_frames, 0)
    grad_action = jnp.dot(action_hot.T, frame_sum, precision=highest) + jnp.dot(
        own_hot.T, own_sum, precision=highest
    )
    grad_v = jnp.concatenate(
        [
            jnp.stack(
                [gain_s, gain_t, gain_f, gain_o, offset_s, offset_t, offset_f, offset_o, grad_mask]
            ),
            grad_action,
        ],
        0,
    )
    vec_count = grad_v.shape[0]
    grad_v = jnp.pad(grad_v, ((0, LANES - vec_count), (0, 0))).T
    vec_part = reducer.start_vector(grad_v)

    owned = [None] * 8
    owned_v = None
    groups = [
        [(7, head_part), (5, down_part)],
        [(4, up_part)],
        [(3, time_out_part), (2, time_in_part)],
        [(1, space_out_part), (0, space_in_part), (6, embed_part), (8, vec_part)],
    ]
    for group in groups:
        summed = reducer.finish([started for _, started in group])
        widths = [started[0] for number, started in group if number < 8]
        wholes = reducer.spread(summed[:, : sum(widths)], widths)
        for (number, _), whole in zip(group, wholes):
            owned[number] = whole
        if group[-1][0] == 8:
            owned_v = summed[:, sum(widths) :][:, :vec_count].T

    rows = weights.shape[0]
    outers = []
    for number in range(8):
        block = owned[number].reshape(rows // BLOCK, BLOCK, WIDTHS[number])
        outers.append(jnp.einsum("bic,bkc->bik", block, block, preferred_element_type=f32))
    outers = jnp.stack(outers)
    diagonal = jnp.eye(BLOCK, dtype=f32)
    squares = jnp.sum(outers * diagonal) + jnp.sum(owned_v * owned_v)
    sums = jnp.concatenate([ce_part, (squares / tiles)[None]])
    for name in ("core", "x", "inner", "outer"):
        sums = levels[name].sum(sums)
    ce_total = sums[:NDOM]
    grad_norm = jnp.sqrt(sums[NDOM])
    clip_scale = 1.0 / jnp.maximum(grad_norm, 1.0)
    new_weights, new_weight_m, new_weight_v = update_weights(
        clip_scale, jnp.concatenate(owned, 1), weights, weight_m, weight_v, bases
    )
    new_stats, new_bases = turn_bases(clip_scale, outers, stats, bases)
    new_vectors, new_vector_m, new_vector_v = adam_update(
        vectors, vector_m, vector_v, owned_v * clip_scale
    )
    loss_terms = jnp.stack([ce_total, counts])
    return (
        loss_terms,
        grad_norm,
        new_weights,
        new_weight_m,
        new_weight_v,
        new_stats,
        new_bases,
        new_vectors,
        new_vector_m,
        new_vector_v,
    )


def solution(mesh):
    sizes = (mesh.shape["clip"], mesh.shape["tile"])
    placed = (
        P("clip", None, "tile"),
        P("clip", None, "tile"),
        P("clip", None),
        P("clip"),
        P("clip", None),
        P("clip", None),
        P("clip", None),
        P(None, "clip", None),
        P(None, "clip", None),
        P(None, "clip"),
        P(None, "clip"),
        P(None, "clip"),
    )
    return jax.shard_map(
        partial(body, sizes),
        mesh=mesh,
        in_specs=placed,
        out_specs=(
            P(),
            P(),
            P("clip", None),
            P("clip", None),
            P("clip", None),
            P(None, "clip", None),
            P(None, "clip", None),
            P(None, "clip"),
            P(None, "clip"),
            P(None, "clip"),
        ),
        check_vma=False,
    )
```

time: 2820 us -> 1100 us (0.39)
  waiting for transfers between devices: 1540 us -> 365 us
  other arithmetic: 313 us -> 74.5 us
  matrix products: 453 us -> 243 us
  blocking collectives: 163 us -> 6.47 us
  local copies, waits for them, and re-layouts: 306 us -> 170 us
  Pallas kernels: 0 us -> 127 us
  starting transfers between devices: 0.71 us -> 84.2 us
    reduce_scatter x2 -> x0, waiting for transfers between devices: 670 us -> none  [the longest x1 588 us: body(): lax.psum_scatter(grad_w.astype(jnp.bfloat16), 'clip', scatter_dimension=0...]
    all_gather x2 -> x3, waiting for transfers between devices: 740 us -> 115 us  [fetch(): whole = lax.all_gather(jnp.concatenate(pieces, 1), both, axis=0, tiled=True)]
    ppermute x0 -> x58, waiting for transfers between devices: none -> 250 us  [the longest x42 217 us: shift(): return lax.ppermute(array, ('clip', 'tile'), pairs)]
    dot_general x84 -> x58, matrix products: 444 us -> 242 us  [the longest x7 84 us: dot_nn(): return jnp.dot(former, latter, preferred_element_type=f32)]
    another operation x28 -> x3, other arithmetic: 200 us -> 8.46 us  [the longest x18 107 us: soap_update(): factor = jnp.linalg.cholesky(gram)]
    pallas_call x0 -> x6, Pallas kernels: none -> 127 us  [the longest x1 29.7 us: update_weights(): pl.pallas_call(update_kernel, grid=(cols // chunk,), in_specs=[pl.BlockSp...]
    psum x1 -> x0, waiting for transfers between devices: 88 us -> none  [body(): lax.psum(owned_w.astype(jnp.bfloat16), 'tile').astype(jnp.float32)]
    psum x3 -> x0, blocking collectives: 85 us -> none  [the longest x2 79.3 us: body(): counts, ce_total = lax.psum((count_part, ce_part), ('clip', 'tile'))]
  transfers between devices with their start and end apart: 6 -> 61, of which waited for: 6 -> 31; matrix products, arithmetic and copies ran while one was open for 3% -> 25% of each run, Pallas kernels for 0% -> 5%
where the time goes in v1:
time: 1100 us; the launch traced here: 1090 us
  waiting for transfers between devices  365 us (33%)
  matrix products  243 us (22%)
  local copies, waits for them, and re-layouts  170 us (15%)
  Pallas kernels  127 us (12%)
  starting transfers between devices  84.2 us (8%)
  other arithmetic  74.5 us (7%)
  between operations  22.2 us (2%)
    ppermute x42, waiting for transfers between devices, shift(): return lax.ppermute(array, ('clip', 'tile'), pairs)  217 us
    all_gather x3, waiting for transfers between devices, fetch(): whole = lax.all_gather(jnp.concatenate(pieces, 1), both, axis=0, tiled=True)  115 us
    dot_general x7, matrix products, dot_nn(): return jnp.dot(former, latter, preferred_element_type=f32)  84 us
    dot_general x32, matrix products, dot_tn(): lax.dot_general(former, latter, (((0,), (0,)), ((), ())), preferred_eleme...  84 us
    dot_general x9, matrix products, dot_nt(): lax.dot_general(former, latter, (((1,), (1,)), ((), ())), preferred_eleme...  70.3 us
    ppermute x42, starting transfers between devices, shift(): return lax.ppermute(array, ('clip', 'tile'), pairs)  62 us
    unnamed x310, local copies, waits for them, and re-layouts  56.3 us
    dynamic_slice x9, local copies, waits for them, and re-layouts, rows_of(): lax.dynamic_index_in_dim(split, inner, 2, keepdims=False)  33.2 us
  transfers between devices with their start and end apart: 61, of which 31 were waited for; matrix products, arithmetic and copies ran while one was open for 25% of the time, Pallas kernels for 5%

profile of v1, /device:TPU:0, one launch (start us, length us, event | category | flops | bytes accessed | tf_op | source)
XLA Modules:
  0.0 1091.6 jit_solution(14052092057070565884)
XLA Ops:
  14.0 6.5 all-gather
  32.5 60.2 %all-gather.5.cloned.1.call-done = bf16[1024,4224]{1,0:T(8,128)(2,1)} async-done(((bf16[32,4224]{1,0:T(8,128)(2,1)}), bf16[1024,4224]{1,0:T(8,128)(2,1)}) %all-gather.5.cloned.1.call-update) | async-done | bytes 8650768 | tf_op jit(solution)/shard_map/all_gather | solution.py:572
  106.2 7.3 convolution_convert_fusion.1.query_ref.key_ref.value_ref
  113.6 16.4 %shard_map.195 = bf16[1024,1024]{1,0:T(8,128)(2,1)S(1)} custom-call(bf16[1024,3072]{1,0:T(8,128)(2,1)S(1)} %convolution_convert_fusion.1.query_ref.key_ref.value_ref, bf16[1024,3072]{1,0:T(8,128)(2,1)S(1)} %convolution_convert_fusion.1.query_ref.key_ref.value_ref, bf16[1024,3072]{1,0:T(8,128)(2,1)S(1)} %convolution_convert_fusion.1.query_ref.key_ref.value_ref), custom_call_target="tpu_custom_call" | custom-call | tf_op jit(solution)/shard_map/pallas_call | solution.py:182
  154.6 12.7 %collective-permute-done.2 = bf16[1,4,64,1024]{3,2,1,0:T(8,128)(2,1)} collective-permute-done((bf16[1,4,64,1024]{3,2,1,0:T(8,128)(2,1)}, bf16[1,4,64,1024]{3,2,1,0:T(8,128)(2,1)}, u32[]{:S(2)}, u32[]{:S(2)}) %collective-permute-start.2) | collective-permute-done | bytes 524320 | tf_op jit(solution)/shard_map/ppermute | solution.py:618
  172.5 6.4 constant_dynamic-slice_fusion.71
  178.9 6.0 copy.305
  190.7 8.0 fusion.234
  201.9 7.3 convolution_convert_fusion
  209.3 16.8 %shard_map.196 = bf16[16,64,1024]{2,1,0:T(8,128)(2,1)S(1)} custom-call(bf16[16,64,3072]{2,1,0:T(8,128)(2,1)S(1)} %bitcast.390, bf16[16,64,3072]{2,1,0:T(8,128)(2,1)S(1)} %bitcast.391, bf16[16,64,3072]{2,1,0:T(8,128)(2,1)S(1)} %bitcast.392), custom_call_target="tpu_custom_call" | custom-call | tf_op jit(solution)/shard_map/pallas_call | solution.py:211
  231.7 8.6 constant_dynamic-slice_fusion.43
  240.3 5.9 copy.374
  246.1 6.0 copy.377
  263.7 53.2 %all-gather.9.cloned.1.call-done = bf16[1024,9216]{1,0:T(8,128)(2,1)} async-done(((bf16[32,9216]{1,0:T(8,128)(2,1)}), bf16[1024,9216]{1,0:T(8,128)(2,1)}) %all-gather.9.cloned.1.call-update) | async-done | bytes 18874384 | tf_op jit(solution)/shard_map/all_gather | solution.py:572
  316.9 25.0 %multiply_convert_fusion.1 = (bf16[1024,4096]{1,0:T(8,128)(2,1)S(1)}, f32[1024,4096]{1,0:T(8,128)}) fusion(bf16[1024,1024]{0,1:T(8,128)(2,1)S(1)} %add_convert_fusion.3, bf16[1024,9216]{1,0:T(8,128)(2,1)} %all-gather.9.cloned.1.call-done), kind=kOutput, calls=%fused_computation.4 | convolution fusion | flops 8686403584 | bytes 35651584 | tf_op jit(solution)/shard_map/dot_general | solution.py:46
  342.0 14.8 %fusion.236 = (f32[1024]{0:T(1024)S(1)}, f32[1024,1024]{0,1:T(8,128)S(1)}) fusion(f32[1024,1024]{0,1:T(8,128)S(1)} %copy-done.13, bf16[1024,4096]{1,0:T(8,128)(2,1)S(1)} %get-tuple-element.233, bf16[1024,9216]{1,0:T(8,128)(2,1)} %all-gather.9.cloned.1.call-done), kind=kOutput, calls=%fused_computation.503 | convolution fusion | flops 8592030720 | bytes 25169920 | tf_op jit(solution)/shard_map/dot_general | solution.py:54
  404.0 6.3 fusion.28
  410.3 26.1 %multiply_convert_fusion = bf16[1024,4096]{1,0:T(8,128)(2,1)S(1)} fusion(f32[1024,4096]{1,0:T(8,128)} %get-tuple-element.234, bf16[1024,1024]{0,1:T(8,128)(2,1)S(1)} %fusion.221, bf16[1024,9216]{1,0:T(8,128)(2,1)} %all-gather.9.cloned.1.call-done), kind=kOutput, calls=%fused_computation.3 | convolution fusion | flops 8698986496 | bytes 35651584 | tf_op jit(solution)/shard_map/dot_general | solution.py:46
  436.4 6.1 fusion.25
  442.5 13.4 %fusion.240 = (f32[1024]{0:T(1024)}, f32[1024,1024]{1,0:T(8,128)}) fusion(bf16[1024,4096]{1,0:T(8,128)(2,1)S(1)} %multiply_convert_fusion, bf16[1024,9216]{1,0:T(8,128)(2,1)} %all-gather.9.cloned.1.call-done), kind=kOutput, calls=%fused_computation.507 | convolution fusion | flops 8590982144 | bytes 20975616 | tf_op jit(solution)/shard_map/dot_general | solution.py:54
  467.3 6.6 fusion.230
  480.1 24.8 %shard_map.197 = (bf16[16,64,1024]{2,1,0:T(8,128)(2,1)S(1)}, bf16[16,64,1024]{2,1,0:T(8,128)(2,1)S(1)}, bf16[16,64,1024]{2,1,0:T(8,128)(2,1)S(1)}) custom-call(bf16[16,64,3072]{2,1,0:T(8,128)(2,1)} %bitcast.393, bf16[16,64,3072]{2,1,0:T(8,128)(2,1)} %bitcast.394, bf16[16,64,3072]{2,1,0:T(8,128)(2,1)} %bitcast.395, bf16[16,64,1024]{2,1,0:T(8,128)(2,1)S(1)} %bitcast.405), custom_call_target="tpu_custom_call" | custom-call | tf_op jit(solution)/shard_map/pallas_call | solution.py:227
  508.5 12.0 %fusion.239 = (f32[1024]{0:T(1024)}, f32[1024,1024]{1,0:T(8,128)}) fusion(bf16[1024,5120]{1,0:T(8,128)(2,1)} %all-gather.7.cloned.1.call-done, bf16[1024,1024]{1,0:T(8,128)(2,1)S(1)} %bitcast.412, bf16[1024,1024]{1,0:T(8,128)(2,1)S(1)} %bitcast.410, bf16[1024,1024]{1,0:T(8,128)(2,1)S(1)} %bitcast.408), kind=kOutput, calls=%fused_computation.506 | convolution fusion | flops 6462372864 | bytes 16781312 | tf_op jit(solution)/shard_map/dot_general | solution.py:54
  569.9 9.8 collective-permute-start.25
  580.1 23.0 %shard_map.198 = (bf16[1024,1024]{1,0:T(8,128)(2,1)S(1)}, bf16[1024,1024]{1,0:T(8,128)(2,1)S(1)}, bf16[1024,1024]{1,0:T(8,128)(2,1)S(1)}) custom-call(bf16[1024,3072]{1,0:T(8,128)(2,1)} %copy-done, bf16[1024,3072]{1,0:T(8,128)(2,1)} %copy-done, bf16[1024,3072]{1,0:T(8,128)(2,1)} %copy-done, bf16[1024,1024]{1,0:T(8,128)(2,1)S(1)} %bitcast.401), custom_call_target="tpu_custom_call" | custom-call | tf_op jit(solution)/shard_map/pallas_call | solution.py:195
  611.7 8.9 fusion.238
  635.8 5.6 reshape.634
  651.5 6.3 fusion.85
  689.6 5.8 collective-permute-done.44
  696.9 9.8 collective-permute-done.26
  708.6 8.3 collective-permute-done.9
  721.7 8.2 collective-permute-done.16
  741.3 6.3 add_convert_fusion
  758.4 14.0 %collective-permute-done.28 = bf16[1024,768]{1,0:T(8,128)(2,1)S(1)} collective-permute-done((bf16[1024,768]{1,0:T(8,128)(2,1)}, bf16[1024,768]{1,0:T(8,128)(2,1)S(1)}, u32[]{:S(2)}, u32[]{:S(2)}) %collective-permute-start.28) | collective-permute-done | bytes 1572896 | tf_op jit(solution)/shard_map/ppermute | solution.py:252
  776.9 29.2 %collective-permute-done.14 = bf16[1024,768]{1,0:T(8,128)(2,1)S(1)} collective-permute-done((bf16[1024,768]{1,0:T(8,128)(2,1)}, bf16[1024,768]{1,0:T(8,128)(2,1)S(1)}, u32[]{:S(2)}, u32[]{:S(2)}) %collective-permute-start.14) | collective-permute-done | bytes 1572896 | tf_op jit(solution)/shard_map/ppermute | solution.py:252
  813.8 5.7 collective-permute-done.30
  827.0 24.0 %collective-permute-done.46 = bf16[1024,1024]{1,0:T(8,128)(2,1)S(1)} collective-permute-done((bf16[1024,1024]{1,0:T(8,128)(2,1)}, bf16[1024,1024]{1,0:T(8,128)(2,1)S(1)}, u32[]{:S(2)}, u32[]{:S(2)}) %collective-permute-start.46) | collective-permute-done | bytes 2097184 | tf_op jit(solution)/shard_map/ppermute | solution.py:252
  854.5 41.5 %collective-permute-done.36 = bf16[1024,1024]{1,0:T(8,128)(2,1)S(1)} collective-permute-done((bf16[1024,1024]{1,0:T(8,128)(2,1)S(1)}, bf16[1024,1024]{1,0:T(8,128)(2,1)S(1)}, u32[]{:S(2)}, u32[]{:S(2)}) %collective-permute-start.36) | collective-permute-done | bytes 2097184 | tf_op jit(solution)/shard_map/ppermute | solution.py:252
  907.9 8.7 collective-permute-done.20
  916.6 14.6 %collective-permute-done.21 = bf16[128,1408]{1,0:T(8,128)(2,1)S(1)} collective-permute-done((bf16[128,1408]{1,0:T(8,128)(2,1)S(1)}, bf16[128,1408]{1,0:T(8,128)(2,1)S(1)}, u32[]{:S(2)}, u32[]{:S(2)}) %collective-permute-start.21) | collective-permute-done | bytes 360480 | tf_op jit(solution)/shard_map/ppermute | solution.py:252
  933.9 7.9 collective-permute-start.38
  949.9 9.9 collective-permute-done.39
  962.0 6.1 collective-permute-start.48
  970.9 6.9 collective-permute-done.48
  977.8 11.7 %collective-permute-done.49 = bf16[128,1280]{1,0:T(8,128)(2,1)S(1)} collective-permute-done((bf16[128,1280]{1,0:T(8,128)(2,1)S(1)}, bf16[128,1280]{1,0:T(8,128)(2,1)S(1)}, u32[]{:S(2)}, u32[]{:S(2)}) %collective-permute-start.49) | collective-permute-done | bytes 327712 | tf_op jit(solution)/shard_map/ppermute | solution.py:252
  1015.9 7.6 collective-permute-start.56
  1033.8 15.7 %shard_map.200 = (f32[16,64,64]{2,1,0:T(8,128)S(1)}, f32[16,64,64]{2,1,0:T(8,128)S(1)}) custom-call(f32[1]{0:T(128)} %bitcast.125.scale_ref, f32[16,64,64]{2,1,0:T(8,128)S(1)} %bitcast.404, f32[16,64,64]{2,1,0:T(8,128)S(1)} %bitcast.406, f32[16,64,64]{2,1,0:T(8,128)S(1)} %bitcast.403), custom_call_target="tpu_custom_call" | custom-call | tf_op jit(solution)/shard_map/pallas_call | solution.py:516
  1053.7 29.7 %shard_map.199 = (f32[128,18432]{1,0:T(8,128)}, f32[128,18432]{1,0:T(8,128)}, f32[128,18432]{1,0:T(8,128)}) custom-call(f32[1]{0:T(128)} %bitcast.125.scale_ref, bf16[128,18432]{1,0:T(8,128)(2,1)} %constant_dynamic-update-slice_fusion.20.grad_ref, f32[128,18432]{1,0:T(8,128)} %weight_ref.1, f32[128,18432]{1,0:T(8,128)} %moment_ref.1, ...), custom_call_target="tpu_custom_call" | custom-call | tf_op jit(solution)/shard_map/pallas_call | solution.py:456
  (686 shorter events, 387.4 us)
Async XLA Ops:
  7.2 85.5 %all-gather.5.cloned.1.call-start = ((), (), s32[]{:S(2)}) async-start(), calls=%async_computation | async-start | bytes 8921088 | tf_op jit(solution)/shard_map/all_gather | solution.py:572
  10.9 179.9 %all-gather.7.cloned.1.call-start = ((), (), s32[]{:S(2)}) async-start(), calls=%async_computation.1 | async-start | bytes 10813440 | tf_op jit(solution)/shard_map/all_gather | solution.py:572
  11.7 305.2 %all-gather.9.cloned.1.call-start = ((), (), s32[]{:S(2)}) async-start(), calls=%async_computation.2 | async-start | bytes 19464192 | tf_op jit(solution)/shard_map/all_gather | solution.py:572
  131.3 19.6 %collective-permute-start = (bf16[1,4,64,1024]{3,2,1,0:T(8,128)(2,1)}, bf16[1,4,64,1024]{3,2,1,0:T(8,128)(2,1)}, u32[]{:S(2)}, u32[]{:S(2)}) collective-permute-start(bf16[1,4,64,1024]{3,2,1,0:T(8,128)(2,1)} %get-tuple-element.175), channel_id=1, source_target_pairs={{0,1},{1,2},{2,3},{3,0},{4,5},{5,6},{6,7},{7,4},{8,9},{9,10},{10,1... | collective-permute-start | bytes 1572872 | tf_op jit(solution)/shard_map/ppermute | solution.py:618
  131.5 21.2 %collective-permute-start.1 = (bf16[1,4,64,1024]{3,2,1,0:T(8,128)(2,1)}, bf16[1,4,64,1024]{3,2,1,0:T(8,128)(2,1)}, u32[]{:S(2)}, u32[]{:S(2)}) collective-permute-start(bf16[1,4,64,1024]{3,2,1,0:T(8,128)(2,1)} %get-tuple-element.174), channel_id=1, source_target_pairs={{0,2},{1,3},{2,0},{3,1},{4,6},{5,7},{6,4},{7,5},{8,10},{9,11},{10,... | collective-permute-start | bytes 1572872 | tf_op jit(solution)/shard_map/ppermute | solution.py:618
  133.0 34.4 %collective-permute-start.2 = (bf16[1,4,64,1024]{3,2,1,0:T(8,128)(2,1)}, bf16[1,4,64,1024]{3,2,1,0:T(8,128)(2,1)}, u32[]{:S(2)}, u32[]{:S(2)}) collective-permute-start(bf16[1,4,64,1024]{3,2,1,0:T(8,128)(2,1)} %get-tuple-element.173), channel_id=1, source_target_pairs={{0,3},{1,0},{2,1},{3,2},{4,7},{5,4},{6,5},{7,6},{8,11},{9,8},{10,9... | collective-permute-start | bytes 1572872 | tf_op jit(solution)/shard_map/ppermute | solution.py:618
  545.6 130.6 %collective-permute-start.43 = (bf16[1024,512]{1,0:T(8,128)(2,1)}, bf16[1024,512]{1,0:T(8,128)(2,1)}, u32[]{:S(2)}, u32[]{:S(2)}) collective-permute-start(bf16[1024,512]{1,0:T(8,128)(2,1)} %convolution_convert_fusion.6), channel_id=1, source_target_pairs={{0,1},{1,0},{2,3},{3,2},{4,5},{5,4},{6,7},{7,6},{8,9},{9,8},{10,11... | collective-permute-start | bytes 3145736 | tf_op jit(solution)/shard_map/ppermute | solution.py:252
  545.6 195.6 %collective-permute-start.45 = (bf16[1024,2048]{1,0:T(8,128)(2,1)}, bf16[1024,2048]{1,0:T(8,128)(2,1)}, u32[]{:S(2)}, u32[]{:S(2)}) collective-permute-start(bf16[1024,2048]{1,0:T(8,128)(2,1)} %fusion.28), channel_id=1, source_target_pairs={{0,1},{1,0},{2,3},{3,2},{4,5},{5,4},{6,7},{7,6},{8,9},{9,8},{10,11... | collective-permute-start | bytes 12582920 | tf_op jit(solution)/shard_map/ppermute | solution.py:252
  555.0 14.8 %collective-permute-start.10 = (bf16[1,4,64,1024]{3,2,1,0:T(8,128)(2,1)S(1)}, bf16[1,4,64,1024]{3,2,1,0:T(8,128)(2,1)S(1)}, u32[]{:S(2)}, u32[]{:S(2)}) collective-permute-start(bf16[1,4,64,1024]{3,2,1,0:T(8,128)(2,1)S(1)} %get-tuple-element.171), channel_id=1, source_target_pairs={{0,1},{1,2},{2,3},{3,0},{4,5},{5,6},{6,7},{7,4},{8,9},{9,10},{10,1... | collective-permute-start | bytes 1572872 | tf_op jit(solution)/shard_map/ppermute | solution.py:618
  555.1 14.8 %collective-permute-start.11 = (bf16[1,4,64,1024]{3,2,1,0:T(8,128)(2,1)S(1)}, bf16[1,4,64,1024]{3,2,1,0:T(8,128)(2,1)S(1)}, u32[]{:S(2)}, u32[]{:S(2)}) collective-permute-start(bf16[1,4,64,1024]{3,2,1,0:T(8,128)(2,1)S(1)} %get-tuple-element.170), channel_id=1, source_target_pairs={{0,2},{1,3},{2,0},{3,1},{4,6},{5,7},{6,4},{7,5},{8,10},{9,11},{10,... | collective-permute-start | bytes 1572872 | tf_op jit(solution)/shard_map/ppermute | solution.py:618
  556.6 23.2 %collective-permute-start.12 = (bf16[1,4,64,1024]{3,2,1,0:T(8,128)(2,1)S(1)}, bf16[1,4,64,1024]{3,2,1,0:T(8,128)(2,1)S(1)}, u32[]{:S(2)}, u32[]{:S(2)}) collective-permute-start(bf16[1,4,64,1024]{3,2,1,0:T(8,128)(2,1)S(1)} %get-tuple-element.169), channel_id=1, source_target_pairs={{0,3},{1,0},{2,1},{3,2},{4,7},{5,4},{6,5},{7,6},{8,11},{9,8},{10,9... | collective-permute-start | bytes 1572872 | tf_op jit(solution)/shard_map/ppermute | solution.py:618
  569.9 178.8 %collective-permute-start.35 = (bf16[1024,2048]{1,0:T(8,128)(2,1)}, bf16[1024,2048]{1,0:T(8,128)(2,1)}, u32[]{:S(2)}, u32[]{:S(2)}) collective-permute-start(bf16[1024,2048]{1,0:T(8,128)(2,1)} %fusion.25), channel_id=1, source_target_pairs={{0,1},{1,0},{2,3},{3,2},{4,5},{5,4},{6,7},{7,6},{8,9},{9,8},{10,11... | collective-permute-start | bytes 12582920 | tf_op jit(solution)/shard_map/ppermute | solution.py:252
  569.9 110.6 %collective-permute-start.25 = (bf16[1024,512]{1,0:T(8,128)(2,1)}, bf16[1024,512]{1,0:T(8,128)(2,1)}, u32[]{:S(2)}, u32[]{:S(2)}) collective-permute-start(bf16[1024,512]{1,0:T(8,128)(2,1)} %convolution_convert_fusion.7), channel_id=1, source_target_pairs={{0,1},{1,0},{2,3},{3,2},{4,5},{5,4},{6,7},{7,6},{8,9},{9,8},{10,11... | collective-permute-start | bytes 3145736 | tf_op jit(solution)/shard_map/ppermute | solution.py:252
  666.1 19.0 %collective-permute-start.8 = (bf16[1024,512]{1,0:T(8,128)(2,1)}, bf16[1024,512]{1,0:T(8,128)(2,1)}, u32[]{:S(2)}, u32[]{:S(2)}) collective-permute-start(bf16[1024,512]{1,0:T(8,128)(2,1)} %convolution_convert_fusion.8), channel_id=1, source_target_pairs={{0,1},{1,0},{2,3},{3,2},{4,5},{5,4},{6,7},{7,6},{8,9},{9,8},{10,11... | collective-permute-start | bytes 3145736 | tf_op jit(solution)/shard_map/ppermute | solution.py:252
  676.2 30.6 %collective-permute-start.15 = (bf16[1024,512]{1,0:T(8,128)(2,1)}, bf16[1024,512]{1,0:T(8,128)(2,1)S(1)}, u32[]{:S(2)}, u32[]{:S(2)}) collective-permute-start(bf16[1024,512]{1,0:T(8,128)(2,1)} %fusion.85), channel_id=1, source_target_pairs={{0,1},{1,0},{2,3},{3,2},{4,5},{5,4},{6,7},{7,6},{8,9},{9,8},{10,11... | collective-permute-start | bytes 3145736 | tf_op jit(solution)/shard_map/ppermute | solution.py:252
  680.6 14.9 %collective-permute-start.44 = (bf16[1024,256]{1,0:T(8,128)(2,1)S(1)}, bf16[1024,256]{1,0:T(8,128)(2,1)S(1)}, u32[]{:S(2)}, u32[]{:S(2)}) collective-permute-start(bf16[1024,256]{1,0:T(8,128)(2,1)S(1)} %add_convert_fusion.8), channel_id=1, source_target_pairs={{0,2},{1,3},{2,0},{3,1},{4,6},{5,7},{6,4},{7,5},{8,10},{9,11},{10,... | collective-permute-start | bytes 1572872 | tf_op jit(solution)/shard_map/ppermute | solution.py:252
  685.2 21.5 %collective-permute-start.26 = (bf16[1024,256]{1,0:T(8,128)(2,1)S(1)}, bf16[1024,256]{1,0:T(8,128)(2,1)S(1)}, u32[]{:S(2)}, u32[]{:S(2)}) collective-permute-start(bf16[1024,256]{1,0:T(8,128)(2,1)S(1)} %add_convert_fusion.9), channel_id=1, source_target_pairs={{0,2},{1,3},{2,0},{3,1},{4,6},{5,7},{6,4},{7,5},{8,10},{9,11},{10,... | collective-permute-start | bytes 1572872 | tf_op jit(solution)/shard_map/ppermute | solution.py:252
  695.4 21.5 %collective-permute-start.9 = (bf16[1024,256]{1,0:T(8,128)(2,1)S(1)}, bf16[1024,256]{1,0:T(8,128)(2,1)S(1)}, u32[]{:S(2)}, u32[]{:S(2)}) collective-permute-start(bf16[1024,256]{1,0:T(8,128)(2,1)S(1)} %fusion.96), channel_id=1, source_target_pairs={{0,2},{1,3},{2,0},{3,1},{4,6},{5,7},{6,4},{7,5},{8,10},{9,11},{10,... | collective-permute-start | bytes 1572872 | tf_op jit(solution)/shard_map/ppermute | solution.py:252
  706.6 25.1 %collective-permute-start.27 = (bf16[1024,1536]{1,0:T(8,128)(2,1)}, bf16[1024,1536]{1,0:T(8,128)(2,1)S(1)}, u32[]{:S(2)}, u32[]{:S(2)}) collective-permute-start(bf16[1024,1536]{1,0:T(8,128)(2,1)} %convolution_convert_fusion.2), channel_id=1, source_target_pairs={{0,1},{1,0},{2,3},{3,2},{4,5},{5,4},{6,7},{7,6},{8,9},{9,8},{10,11... | collective-permute-start | bytes 9437192 | tf_op jit(solution)/shard_map/ppermute | solution.py:252
  706.7 29.8 %collective-permute-start.13 = (bf16[1024,1536]{1,0:T(8,128)(2,1)}, bf16[1024,1536]{1,0:T(8,128)(2,1)S(1)}, u32[]{:S(2)}, u32[]{:S(2)}) collective-permute-start(bf16[1024,1536]{1,0:T(8,128)(2,1)} %convolution_convert_fusion.3), channel_id=1, source_target_pairs={{0,1},{1,0},{2,3},{3,2},{4,5},{5,4},{6,7},{7,6},{8,9},{9,8},{10,11... | collective-permute-start | bytes 9437192 | tf_op jit(solution)/shard_map/ppermute | solution.py:252
  716.9 13.0 %collective-permute-start.16 = (bf16[1024,256]{1,0:T(8,128)(2,1)S(1)}, bf16[1024,256]{1,0:T(8,128)(2,1)S(1)}, u32[]{:S(2)}, u32[]{:S(2)}) collective-permute-start(bf16[1024,256]{1,0:T(8,128)(2,1)S(1)} %add_convert_fusion.10), channel_id=1, source_target_pairs={{0,2},{1,3},{2,0},{3,1},{4,6},{5,7},{6,4},{7,5},{8,10},{9,11},{10,... | collective-permute-start | bytes 1572872 | tf_op jit(solution)/shard_map/ppermute | solution.py:252
  734.9 37.5 %collective-permute-start.28 = (bf16[1024,768]{1,0:T(8,128)(2,1)}, bf16[1024,768]{1,0:T(8,128)(2,1)S(1)}, u32[]{:S(2)}, u32[]{:S(2)}) collective-permute-start(bf16[1024,768]{1,0:T(8,128)(2,1)} %add_convert_fusion.6), channel_id=1, source_target_pairs={{0,2},{1,3},{2,0},{3,1},{4,6},{5,7},{6,4},{7,5},{8,10},{9,11},{10,... | collective-permute-start | bytes 4718600 | tf_op jit(solution)/shard_map/ppermute | solution.py:252
  739.7 66.5 %collective-permute-start.14 = (bf16[1024,768]{1,0:T(8,128)(2,1)}, bf16[1024,768]{1,0:T(8,128)(2,1)S(1)}, u32[]{:S(2)}, u32[]{:S(2)}) collective-permute-start(bf16[1024,768]{1,0:T(8,128)(2,1)} %add_convert_fusion.7), channel_id=1, source_target_pairs={{0,2},{1,3},{2,0},{3,1},{4,6},{5,7},{6,4},{7,5},{8,10},{9,11},{10,... | collective-permute-start | bytes 4718600 | tf_op jit(solution)/shard_map/ppermute | solution.py:252
  747.5 103.5 %collective-permute-start.46 = (bf16[1024,1024]{1,0:T(8,128)(2,1)}, bf16[1024,1024]{1,0:T(8,128)(2,1)S(1)}, u32[]{:S(2)}, u32[]{:S(2)}) collective-permute-start(bf16[1024,1024]{1,0:T(8,128)(2,1)} %add_convert_fusion), channel_id=1, source_target_pairs={{0,2},{1,3},{2,0},{3,1},{4,6},{5,7},{6,4},{7,5},{8,10},{9,11},{10,... | collective-permute-start | bytes 6291464 | tf_op jit(solution)/shard_map/ppermute | solution.py:252
  753.5 142.5 %collective-permute-start.36 = (bf16[1024,1024]{1,0:T(8,128)(2,1)S(1)}, bf16[1024,1024]{1,0:T(8,128)(2,1)S(1)}, u32[]{:S(2)}, u32[]{:S(2)}) collective-permute-start(bf16[1024,1024]{1,0:T(8,128)(2,1)S(1)} %add_convert_fusion.1), channel_id=1, source_target_pairs={{0,2},{1,3},{2,0},{3,1},{4,6},{5,7},{6,4},{7,5},{8,10},{9,11},{10,... | collective-permute-start | bytes 6291464 | tf_op jit(solution)/shard_map/ppermute | solution.py:252
  773.9 34.8 %collective-permute-start.29 = (bf16[512,1024]{1,0:T(8,128)(2,1)S(1)}, bf16[512,1024]{1,0:T(8,128)(2,1)S(1)}, u32[]{:S(2)}, u32[]{:S(2)}) collective-permute-start(bf16[512,1024]{1,0:T(8,128)(2,1)S(1)} %pad_maximum_fusion.8), channel_id=1, source_target_pairs={{0,4},{1,5},{2,6},{3,7},{4,0},{5,1},{6,2},{7,3},{8,12},{9,13},{10,... | collective-permute-start | bytes 3145736 | tf_op jit(solution)/shard_map/ppermute | solution.py:252
  809.2 10.3 collective-permute-start.30
  809.4 15.8 %collective-permute-start.31 = (bf16[128,1024]{1,0:T(8,128)(2,1)S(1)}, bf16[128,1024]{1,0:T(8,128)(2,1)S(1)}, u32[]{:S(2)}, u32[]{:S(2)}) collective-permute-start(bf16[128,1024]{1,0:T(8,128)(2,1)S(1)} %get-tuple-element.197), channel_id=1, source_target_pairs={{0,16},{1,17},{2,18},{3,19},{4,20},{5,21},{6,22},{7,23},{8,24},{9,... | collective-permute-start | bytes 786440 | tf_op jit(solution)/shard_map/ppermute | solution.py:252
  811.3 14.0 %collective-permute-start.32 = (bf16[128,1024]{1,0:T(8,128)(2,1)S(1)}, bf16[128,1024]{1,0:T(8,128)(2,1)S(1)}, u32[]{:S(2)}, u32[]{:S(2)}) collective-permute-start(bf16[128,1024]{1,0:T(8,128)(2,1)S(1)} %get-tuple-element.196), channel_id=1, source_target_pairs={{0,24},{1,25},{2,26},{3,27},{4,28},{5,29},{6,30},{7,31},{8,0},{9,1... | collective-permute-start | bytes 786440 | tf_op jit(solution)/shard_map/ppermute | solution.py:252
  819.5 83.4 %collective-permute-start.19 = (bf16[512,1408]{1,0:T(8,128)(2,1)S(1)}, bf16[512,1408]{1,0:T(8,128)(2,1)S(1)}, u32[]{:S(2)}, u32[]{:S(2)}) collective-permute-start(bf16[512,1408]{1,0:T(8,128)(2,1)S(1)} %pad_maximum_fusion.6), channel_id=1, source_target_pairs={{0,4},{1,5},{2,6},{3,7},{4,0},{5,1},{6,2},{7,3},{8,12},{9,13},{10,... | collective-permute-start | bytes 4325384 | tf_op jit(solution)/shard_map/ppermute | solution.py:252
  825.4 77.1 %collective-permute-start.33 = (bf16[128,1024]{1,0:T(8,128)(2,1)S(1)}, bf16[128,1024]{1,0:T(8,128)(2,1)S(1)}, u32[]{:S(2)}, u32[]{:S(2)}) collective-permute-start(bf16[128,1024]{1,0:T(8,128)(2,1)S(1)} %add_convert_fusion.13), channel_id=1, source_target_pairs={{0,2},{1,3},{2,0},{3,1},{4,6},{5,7},{6,4},{7,5},{8,10},{9,11},{10,... | collective-permute-start | bytes 786440 | tf_op jit(solution)/shard_map/ppermute | solution.py:252
  853.0 108.6 %collective-permute-start.47 = (bf16[512,1280]{1,0:T(8,128)(2,1)S(1)}, bf16[512,1280]{1,0:T(8,128)(2,1)S(1)}, u32[]{:S(2)}, u32[]{:S(2)}) collective-permute-start(bf16[512,1280]{1,0:T(8,128)(2,1)S(1)} %pad_maximum_fusion.7), channel_id=1, source_target_pairs={{0,4},{1,5},{2,6},{3,7},{4,0},{5,1},{6,2},{7,3},{8,12},{9,13},{10,... | collective-permute-start | bytes 3932168 | tf_op jit(solution)/shard_map/ppermute | solution.py:252
  899.5 33.3 %collective-permute-start.37 = (bf16[512,1024]{1,0:T(8,128)(2,1)S(1)}, bf16[512,1024]{1,0:T(8,128)(2,1)S(1)}, u32[]{:S(2)}, u32[]{:S(2)}) collective-permute-start(bf16[512,1024]{1,0:T(8,128)(2,1)S(1)} %fusion.43), channel_id=1, source_target_pairs={{0,4},{1,5},{2,6},{3,7},{4,0},{5,1},{6,2},{7,3},{8,12},{9,13},{10,... | collective-permute-start | bytes 3145736 | tf_op jit(solution)/shard_map/ppermute | solution.py:252
  903.4 13.2 %collective-permute-start.20 = (bf16[128,1408]{1,0:T(8,128)(2,1)S(1)}, bf16[128,1408]{1,0:T(8,128)(2,1)S(1)}, u32[]{:S(2)}, u32[]{:S(2)}) collective-permute-start(bf16[128,1408]{1,0:T(8,128)(2,1)S(1)} %get-tuple-element.184), channel_id=1, source_target_pairs={{0,8},{1,9},{2,10},{3,11},{4,12},{5,13},{6,14},{7,15},{8,16},{9,17... | collective-permute-start | bytes 1081352 | tf_op jit(solution)/shard_map/ppermute | solution.py:252
  903.6 27.6 %collective-permute-start.21 = (bf16[128,1408]{1,0:T(8,128)(2,1)S(1)}, bf16[128,1408]{1,0:T(8,128)(2,1)S(1)}, u32[]{:S(2)}, u32[]{:S(2)}) collective-permute-start(bf16[128,1408]{1,0:T(8,128)(2,1)S(1)} %get-tuple-element.186), channel_id=1, source_target_pairs={{0,16},{1,17},{2,18},{3,19},{4,20},{5,21},{6,22},{7,23},{8,24},{9,... | collective-permute-start | bytes 1081352 | tf_op jit(solution)/shard_map/ppermute | solution.py:252
  905.4 25.8 %collective-permute-start.22 = (bf16[128,1408]{1,0:T(8,128)(2,1)S(1)}, bf16[128,1408]{1,0:T(8,128)(2,1)S(1)}, u32[]{:S(2)}, u32[]{:S(2)}) collective-permute-start(bf16[128,1408]{1,0:T(8,128)(2,1)S(1)} %get-tuple-element.185), channel_id=1, source_target_pairs={{0,24},{1,25},{2,26},{3,27},{4,28},{5,29},{6,30},{7,31},{8,0},{9,1... | collective-permute-start | bytes 1081352 | tf_op jit(solution)/shard_map/ppermute | solution.py:252
  931.4 13.0 %collective-permute-start.23 = (bf16[128,1280]{1,0:T(8,128)(2,1)S(1)}, bf16[128,1280]{1,0:T(8,128)(2,1)S(1)}, u32[]{:S(2)}, u32[]{:S(2)}) collective-permute-start(bf16[128,1280]{1,0:T(8,128)(2,1)S(1)} %slice.239), channel_id=1, source_target_pairs={{0,2},{1,3},{2,0},{3,1},{4,6},{5,7},{6,4},{7,5},{8,10},{9,11},{10,... | collective-permute-start | bytes 983048 | tf_op jit(solution)/shard_map/ppermute | solution.py:252
  933.9 16.0 %collective-permute-start.38 = (bf16[128,1024]{1,0:T(8,128)(2,1)S(1)}, bf16[128,1024]{1,0:T(8,128)(2,1)S(1)}, u32[]{:S(2)}, u32[]{:S(2)}) collective-permute-start(bf16[128,1024]{1,0:T(8,128)(2,1)S(1)} %get-tuple-element.192), channel_id=1, source_target_pairs={{0,8},{1,9},{2,10},{3,11},{4,12},{5,13},{6,14},{7,15},{8,16},{9,17... | collective-permute-start | bytes 786440 | tf_op jit(solution)/shard_map/ppermute | solution.py:252
  941.7 18.1 %collective-permute-start.39 = (bf16[128,1024]{1,0:T(8,128)(2,1)S(1)}, bf16[128,1024]{1,0:T(8,128)(2,1)S(1)}, u32[]{:S(2)}, u32[]{:S(2)}) collective-permute-start(bf16[128,1024]{1,0:T(8,128)(2,1)S(1)} %get-tuple-element.194), channel_id=1, source_target_pairs={{0,16},{1,17},{2,18},{3,19},{4,20},{5,21},{6,22},{7,23},{8,24},{9,... | collective-permute-start | bytes 786440 | tf_op jit(solution)/shard_map/ppermute | solution.py:252
  943.1 16.7 %collective-permute-start.40 = (bf16[128,1024]{1,0:T(8,128)(2,1)S(1)}, bf16[128,1024]{1,0:T(8,128)(2,1)S(1)}, u32[]{:S(2)}, u32[]{:S(2)}) collective-permute-start(bf16[128,1024]{1,0:T(8,128)(2,1)S(1)} %get-tuple-element.193), channel_id=1, source_target_pairs={{0,24},{1,25},{2,26},{3,27},{4,28},{5,29},{6,30},{7,31},{8,0},{9,1... | collective-permute-start | bytes 786440 | tf_op jit(solution)/shard_map/ppermute | solution.py:252
  944.6 45.9 %collective-permute-start.24 = (bf16[128,2560]{1,0:T(8,128)(2,1)S(1)}, bf16[128,2560]{1,0:T(8,128)(2,1)S(1)}, u32[]{:S(2)}, u32[]{:S(2)}) collective-permute-start(bf16[128,2560]{1,0:T(8,128)(2,1)S(1)} %pad_maximum_fusion.9), channel_id=1, source_target_pairs={{0,1},{1,0},{2,3},{3,2},{4,5},{5,4},{6,7},{7,6},{8,9},{9,8},{10,11... | collective-permute-start | bytes 1966088 | tf_op jit(solution)/shard_map/ppermute | solution.py:252
  960.0 10.6 collective-permute-start.41
  962.0 15.8 %collective-permute-start.48 = (bf16[128,1280]{1,0:T(8,128)(2,1)S(1)}, bf16[128,1280]{1,0:T(8,128)(2,1)S(1)}, u32[]{:S(2)}, u32[]{:S(2)}) collective-permute-start(bf16[128,1280]{1,0:T(8,128)(2,1)S(1)} %get-tuple-element.187), channel_id=1, source_target_pairs={{0,8},{1,9},{2,10},{3,11},{4,12},{5,13},{6,14},{7,15},{8,16},{9,17... | collective-permute-start | bytes 983048 | tf_op jit(solution)/shard_map/ppermute | solution.py:252
  968.2 21.4 %collective-permute-start.49 = (bf16[128,1280]{1,0:T(8,128)(2,1)S(1)}, bf16[128,1280]{1,0:T(8,128)(2,1)S(1)}, u32[]{:S(2)}, u32[]{:S(2)}) collective-permute-start(bf16[128,1280]{1,0:T(8,128)(2,1)S(1)} %get-tuple-element.189), channel_id=1, source_target_pairs={{0,16},{1,17},{2,18},{3,19},{4,20},{5,21},{6,22},{7,23},{8,24},{9,... | collective-permute-start | bytes 983048 | tf_op jit(solution)/shard_map/ppermute | solution.py:252
  969.6 20.0 %collective-permute-start.50 = (bf16[128,1280]{1,0:T(8,128)(2,1)S(1)}, bf16[128,1280]{1,0:T(8,128)(2,1)S(1)}, u32[]{:S(2)}, u32[]{:S(2)}) collective-permute-start(bf16[128,1280]{1,0:T(8,128)(2,1)S(1)} %get-tuple-element.188), channel_id=1, source_target_pairs={{0,24},{1,25},{2,26},{3,27},{4,28},{5,29},{6,30},{7,31},{8,0},{9,1... | collective-permute-start | bytes 983048 | tf_op jit(solution)/shard_map/ppermute | solution.py:252
  970.7 29.1 %collective-permute-start.42 = (bf16[128,2048]{1,0:T(8,128)(2,1)S(1)}, bf16[128,2048]{1,0:T(8,128)(2,1)S(1)}, u32[]{:S(2)}, u32[]{:S(2)}) collective-permute-start(bf16[128,2048]{1,0:T(8,128)(2,1)S(1)} %constant_dynamic-update-slice_fusion.4), channel_id=1, source_target_pairs={{0,1},{1,0},{2,3},{3,2},{4,5},{5,4},{6,7},{7,6},{8,9},{9,8},{10,11... | collective-permute-start | bytes 1572872 | tf_op jit(solution)/shard_map/ppermute | solution.py:252
  989.8 9.6 collective-permute-start.51
  1015.9 9.1 collective-permute-start.56
  (155 other events, 2267.0 us)
Sparse Core Ops, SparseCore 0:
  11.5 81.1 all-gather.4
  95.5 95.1 all-gather.6
  193.6 123.2 all-gather.8
